TPU v7x, 128 devices: a whole 4x4x4 slice. The times are simulated.
128 devices in a mesh: row: 4 (over y_hi, core), col: 4 (over z), rep: 8 (over x, y_lo).
Axes of the slice: x: 4, y: 4 (y_hi: 2, y_lo: 2; y = y_hi * 2 + y_lo), z: 4, core: 2. Of those that a mesh axis runs over, the one named last changes fastest.
Arguments:
- features: bfloat16 [32768, 512], P(('row', 'col', 'rep')), may hold values from -6 to 6
- weight: bfloat16 [512, 512], replicated, may hold values from -0.25 to 0.25
- tile_values: bfloat16 [24576, 128, 128], P(('row', 'col', 'rep')), as said below
- tile_rows: int32 [24576], P(('row', 'col', 'rep')), may hold values from 0 to 63
- tile_cols: int32 [24576], P(('row', 'col', 'rep')), may hold values from 0 to 7
- tile_count: int32 [128], P(('row', 'col', 'rep')), may hold values from 48 to 192, as said below
- output_grad: bfloat16 [32768, 512], P(('row', 'col', 'rep')), may hold values from -6 to 6
Outputs:
- output: bfloat16 [32768, 512], P(('row', 'col', 'rep'))
- grad_features: bfloat16 [32768, 512], P(('row', 'col', 'rep'))
- grad_weight: float32 [512, 512], replicated
Inputs may be any that keep to these rules, and one draw needn't show every extreme that they name: The live tiles of a device are the first tile_count of its 192 slots; in every draw some device has all 192 slots live. `tile_values`: entries are zero or positive.
All inputs are finite; a program needn't handle non-finite values.
Results may differ from a plain program's by a relative error of at most 0.0056.
Values may be sent and summed in bfloat16 or wider, within the bound.
A program may use at most 128 MiB of HBM per device.

v0:
```python
import math

import jax
import jax.numpy as jnp
from jax import lax
from jax.sharding import PartitionSpec as P


def aggregate(values, rows, cols, source, count):
    tiles, tile, _ = values.shape
    width = source.shape[2]
    block = math.gcd(tiles, 32)

    def aggregate_step(index, total):
        start = index * block
        block_values = lax.dynamic_slice_in_dim(values, start, block, 0)
        block_rows = lax.dynamic_slice_in_dim(rows, start, block, 0)
        block_cols = lax.dynamic_slice_in_dim(cols, start, block, 0)
        prod = jnp.einsum(
            "tij,tjf->tif", block_values, source[block_cols], preferred_element_type=jnp.float32
        )
        return total.at[block_rows].add(prod)

    return lax.fori_loop(
        0, tiles // block, aggregate_step, jnp.zeros((count, tile, width), jnp.float32)
    )


def spread_back(values, rows, cols, source, count):
    tiles, tile, _ = values.shape
    width = source.shape[2]
    block = math.gcd(tiles, 32)

    def spread_step(index, total):
        start = index * block
        block_values = lax.dynamic_slice_in_dim(values, start, block, 0)
        block_rows = lax.dynamic_slice_in_dim(rows, start, block, 0)
        block_cols = lax.dynamic_slice_in_dim(cols, start, block, 0)
        prod = jnp.einsum(
            "tij,tif->tjf", block_values, source[block_rows], preferred_element_type=jnp.float32
        )
        return total.at[block_cols].add(prod)

    return lax.fori_loop(
        0, tiles // block, spread_step, jnp.zeros((count, tile, width), jnp.float32)
    )


def per_device(features, weight, tile_values, tile_rows, tile_cols, tile_count, output_grad):
    node_dev, width = features.shape
    tiles, tile, _ = tile_values.shape
    projected = jnp.dot(features, weight, preferred_element_type=jnp.float32).astype(jnp.bfloat16)
    live = (jnp.arange(tiles, dtype=jnp.int32) < tile_count[0]).astype(jnp.bfloat16)
    values = tile_values * live[:, None, None]
    column_rows = lax.all_gather(projected, "row", axis=0, tiled=True)
    col_count = column_rows.shape[0] // tile
    row_count = node_dev * lax.axis_size("col") * lax.axis_size("rep") // tile
    partial_value = aggregate(
        values, tile_rows, tile_cols, column_rows.reshape(col_count, tile, width), row_count
    )
    partial_value = partial_value.reshape(row_count * tile, width)
    aggregated = lax.psum_scatter(partial_value, ("col", "rep"), scatter_dimension=0, tiled=True)
    output, pullback = jax.vjp(jax.nn.gelu, aggregated)
    grad_agg = pullback(output_grad.astype(jnp.float32))[0].astype(jnp.bfloat16)
    grid_grads = lax.all_gather(grad_agg, ("col", "rep"), axis=0, tiled=True)
    terms = spread_back(
        values, tile_rows, tile_cols, grid_grads.reshape(row_count, tile, width), col_count
    )
    terms = terms.reshape(col_count * tile, width)
    grad_proj = lax.psum_scatter(terms, "row", scatter_dimension=0, tiled=True)
    grad_features = jnp.dot(
        grad_proj, weight.astype(jnp.float32).T, precision=lax.Precision.HIGHEST
    ).astype(jnp.bfloat16)
    weight_term = jnp.dot(
        features.astype(jnp.float32).T, grad_proj, precision=lax.Precision.HIGHEST
    )
    grad_weight = lax.psum(weight_term, ("row", "col", "rep"))
    return (output.astype(jnp.bfloat16), grad_features, grad_weight)


def solution(mesh):
    return jax.shard_map(
        per_device,
        mesh=mesh,
        in_specs=(
            P(("row", "col", "rep"), None),
            P(),
            P(("row", "col", "rep"), None, None),
            P(("row", "col", "rep")),
            P(("row", "col", "rep")),
            P(("row", "col", "rep")),
            P(("row", "col", "rep"), None),
        ),
        out_specs=(P(("row", "col", "rep"), None), P(("row", "col", "rep"), None), P()),
        check_vma=False,
    )
```

profile of v0, /device:TPU:1, one launch (start us, length us, event | category | flops | bytes accessed | tf_op | source)
XLA Modules:
  0.0 1117.7 jit_solution(234063734346426817)
XLA Ops:
  7.2 1.0 copy-done
  8.2 2.0 convolution_convert_fusion
  10.2 8.5 copy.10
  19.4 6.0 broadcast_multiply_fusion
  25.4 9.3 all-gather.3.cloned.1.call-done
  34.7 7.9 broadcast_in_dim.35
  42.6 171.9 %while.26 = (s32[]{:T(128)}, f32[64,128,512]{2,1,0:T(8,128)}, s32[192]{0:T(256)S(1)}, bf16[192,128,128]{1,2,0:T(8,128)(2,1)}, s32[192]{0:T(256)S(1)}, /*index=5*...) while((s32[]{:T(128)}, f32[64,128,512]{2,1,0:T(8,128)}, s32[192]{0:T(256)S(1)}, ...), condition=%wide.region_2.0_spmd, body=%wide.region_0.0_spmd.sunk | while | flops 538969280 | bytes 47191064 | solution.py:24
  42.7 0.1 compare_select_fusion.6
  42.7 2.8 gather_fusion
  45.5 7.0 fusion.32
  52.5 18.8 %scatter_fusion = f32[64,128,512]{2,1,0:T(8,128)} fusion(f32[64,128,512]{2,1,0:T(8,128)} %get-tuple-element.355, s32[32]{0:T(128)S(1)} %get-tuple-element.334, f32[32,128,512]{2,1,0:T(8,128)} %fusion.32), kind=kCustom, calls=%fused_computation.2.clone.1 | custom fusion | flops 2097152 | bytes 25165952 | tf_op jit(solution)/shard_map/while/body/eval_jaxpr/scatter-add | solution.py:22
  71.3 0.1 compare_select_fusion.6
  71.4 2.8 gather_fusion
  74.2 7.0 fusion.32
  81.2 18.9 %scatter_fusion = f32[64,128,512]{2,1,0:T(8,128)} fusion(f32[64,128,512]{2,1,0:T(8,128)} %get-tuple-element.355, s32[32]{0:T(128)S(1)} %get-tuple-element.334, f32[32,128,512]{2,1,0:T(8,128)} %fusion.32), kind=kCustom, calls=%fused_computation.2.clone.1 | custom fusion | flops 2097152 | bytes 25165952 | tf_op jit(solution)/shard_map/while/body/eval_jaxpr/scatter-add | solution.py:22
  100.1 0.1 compare_select_fusion.6
  100.2 2.8 gather_fusion
  102.9 7.0 fusion.32
  110.0 18.8 %scatter_fusion = f32[64,128,512]{2,1,0:T(8,128)} fusion(f32[64,128,512]{2,1,0:T(8,128)} %get-tuple-element.355, s32[32]{0:T(128)S(1)} %get-tuple-element.334, f32[32,128,512]{2,1,0:T(8,128)} %fusion.32), kind=kCustom, calls=%fused_computation.2.clone.1 | custom fusion | flops 2097152 | bytes 25165952 | tf_op jit(solution)/shard_map/while/body/eval_jaxpr/scatter-add | solution.py:22
  128.8 0.1 compare_select_fusion.6
  128.9 2.8 gather_fusion
  131.7 7.0 fusion.32
  138.7 18.6 %scatter_fusion = f32[64,128,512]{2,1,0:T(8,128)} fusion(f32[64,128,512]{2,1,0:T(8,128)} %get-tuple-element.355, s32[32]{0:T(128)S(1)} %get-tuple-element.334, f32[32,128,512]{2,1,0:T(8,128)} %fusion.32), kind=kCustom, calls=%fused_computation.2.clone.1 | custom fusion | flops 2097152 | bytes 25165952 | tf_op jit(solution)/shard_map/while/body/eval_jaxpr/scatter-add | solution.py:22
  157.4 2.8 gather_fusion
  160.1 7.0 fusion.32
  167.2 18.7 %scatter_fusion = f32[64,128,512]{2,1,0:T(8,128)} fusion(f32[64,128,512]{2,1,0:T(8,128)} %get-tuple-element.355, s32[32]{0:T(128)S(1)} %get-tuple-element.334, f32[32,128,512]{2,1,0:T(8,128)} %fusion.32), kind=kCustom, calls=%fused_computation.2.clone.1 | custom fusion | flops 2097152 | bytes 25165952 | tf_op jit(solution)/shard_map/while/body/eval_jaxpr/scatter-add | solution.py:22
  186.0 2.8 gather_fusion
  188.8 7.0 fusion.32
  195.8 18.8 %scatter_fusion = f32[64,128,512]{2,1,0:T(8,128)} fusion(f32[64,128,512]{2,1,0:T(8,128)} %get-tuple-element.355, s32[32]{0:T(128)S(1)} %get-tuple-element.334, f32[32,128,512]{2,1,0:T(8,128)} %fusion.32), kind=kCustom, calls=%fused_computation.2.clone.1 | custom fusion | flops 2097152 | bytes 25165952 | tf_op jit(solution)/shard_map/while/body/eval_jaxpr/scatter-add | solution.py:22
  214.6 360.9 %reduce-scatter.3.cloned.1.call-done = f32[256,512]{1,0:T(8,128)} async-done(((f32[8192,512]{1,0:T(8,128)}), f32[256,512]{1,0:T(8,128)}) %reduce-scatter.3.cloned.1.call-update) | async-done | bytes 524304 | tf_op jit(solution)/shard_map/reduce_scatter | solution.py:62
  575.5 2.2 fusion.8
  577.8 187.7 %all-gather.5.cloned.1.call-done = bf16[8192,512]{1,0:T(8,128)(2,1)} async-done(((bf16[256,512]{1,0:T(8,128)(2,1)}), bf16[8192,512]{1,0:T(8,128)(2,1)}) %all-gather.5.cloned.1.call-update) | async-done | bytes 8388624 | tf_op jit(solution)/shard_map/all_gather | solution.py:65
  765.5 0.2 broadcast_in_dim.36
  765.8 150.1 %while.27 = (s32[]{:T(128)}, f32[8,128,512]{2,1,0:T(8,128)S(1)}, s32[192]{0:T(256)S(1)}, bf16[192,128,128]{1,2,0:T(8,128)(2,1)}, s32[192]{0:T(256)S(1)}, /*index...) while((s32[]{:T(128)}, f32[8,128,512]{2,1,0:T(8,128)S(1)}, ...), condition=%wide.region_6.0_spmd, body=%wide.region_4.0_spmd.sunk | while | flops 538969280 | bytes 47191064 | solution.py:44
  765.8 0.1 compare_select_fusion.7
  765.9 6.1 gather_fusion.1
  772.0 7.0 fusion.35
  779.0 11.8 %scatter_fusion.1 = f32[8,128,512]{2,1,0:T(8,128)S(1)} fusion(f32[8,128,512]{2,1,0:T(8,128)S(1)} %get-tuple-element.385, s32[32]{0:T(128)S(1)} %get-tuple-element.342, f32[32,128,512]{2,1,0:T(8,128)} %fusion.35), kind=kCustom, calls=%fused_computation.3.clone.1 | custom fusion | flops 2097152 | bytes 25165952 | tf_op jit(solution)/shard_map/while/body/eval_jaxpr/scatter-add | solution.py:42
  790.8 0.1 compare_select_fusion.7
  790.9 6.1 gather_fusion.1
  797.0 7.0 fusion.35
  804.0 11.8 %scatter_fusion.1 = f32[8,128,512]{2,1,0:T(8,128)S(1)} fusion(f32[8,128,512]{2,1,0:T(8,128)S(1)} %get-tuple-element.385, s32[32]{0:T(128)S(1)} %get-tuple-element.342, f32[32,128,512]{2,1,0:T(8,128)} %fusion.35), kind=kCustom, calls=%fused_computation.3.clone.1 | custom fusion | flops 2097152 | bytes 25165952 | tf_op jit(solution)/shard_map/while/body/eval_jaxpr/scatter-add | solution.py:42
  815.8 0.1 compare_select_fusion.7
  815.9 6.1 gather_fusion.1
  822.1 7.0 fusion.35
  829.1 11.7 %scatter_fusion.1 = f32[8,128,512]{2,1,0:T(8,128)S(1)} fusion(f32[8,128,512]{2,1,0:T(8,128)S(1)} %get-tuple-element.385, s32[32]{0:T(128)S(1)} %get-tuple-element.342, f32[32,128,512]{2,1,0:T(8,128)} %fusion.35), kind=kCustom, calls=%fused_computation.3.clone.1 | custom fusion | flops 2097152 | bytes 25165952 | tf_op jit(solution)/shard_map/while/body/eval_jaxpr/scatter-add | solution.py:42
  840.8 0.1 compare_select_fusion.7
  840.9 6.1 gather_fusion.1
  847.1 7.0 fusion.35
  854.0 11.8 %scatter_fusion.1 = f32[8,128,512]{2,1,0:T(8,128)S(1)} fusion(f32[8,128,512]{2,1,0:T(8,128)S(1)} %get-tuple-element.385, s32[32]{0:T(128)S(1)} %get-tuple-element.342, f32[32,128,512]{2,1,0:T(8,128)} %fusion.35), kind=kCustom, calls=%fused_computation.3.clone.1 | custom fusion | flops 2097152 | bytes 25165952 | tf_op jit(solution)/shard_map/while/body/eval_jaxpr/scatter-add | solution.py:42
  865.8 0.1 compare_select_fusion.7
  865.9 6.1 gather_fusion.1
  872.1 7.0 fusion.35
  879.1 11.8 %scatter_fusion.1 = f32[8,128,512]{2,1,0:T(8,128)S(1)} fusion(f32[8,128,512]{2,1,0:T(8,128)S(1)} %get-tuple-element.385, s32[32]{0:T(128)S(1)} %get-tuple-element.342, f32[32,128,512]{2,1,0:T(8,128)} %fusion.35), kind=kCustom, calls=%fused_computation.3.clone.1 | custom fusion | flops 2097152 | bytes 25165952 | tf_op jit(solution)/shard_map/while/body/eval_jaxpr/scatter-add | solution.py:42
  890.8 0.1 compare_select_fusion.7
  890.9 6.1 gather_fusion.1
  897.1 7.0 fusion.35
  904.1 11.8 %scatter_fusion.1 = f32[8,128,512]{2,1,0:T(8,128)S(1)} fusion(f32[8,128,512]{2,1,0:T(8,128)S(1)} %get-tuple-element.385, s32[32]{0:T(128)S(1)} %get-tuple-element.342, f32[32,128,512]{2,1,0:T(8,128)} %fusion.35), kind=kCustom, calls=%fused_computation.3.clone.1 | custom fusion | flops 2097152 | bytes 25165952 | tf_op jit(solution)/shard_map/while/body/eval_jaxpr/scatter-add | solution.py:42
  915.8 1.3 copy-done.1
  917.2 38.6 %reduce-scatter.5.cloned.1.call-done = f32[256,512]{1,0:T(8,128)} async-done(((f32[1024,512]{1,0:T(8,128)}), f32[256,512]{1,0:T(8,128)}) %reduce-scatter.5.cloned.1.call-update) | async-done | bytes 524304 | tf_op jit(solution)/shard_map/reduce_scatter | solution.py:70
  955.8 2.6 convolution_bitcast_fusion
  958.5 2.4 convolution_convert_fusion.1
  960.8 147.8 %all-reduce.2.cloned.1.call-done = f32[512,512]{0,1:T(8,128)} async-done(((f32[512,512]{0,1:T(8,128)}), f32[512,512]{0,1:T(8,128)}) %all-reduce.2.cloned.1.call-update) | async-done | bytes 1048592 | tf_op jit(solution)/shard_map/psum | solution.py:77
  1108.6 2.5 copy.12
  (37 shorter events, 0.6 us)
Async XLA Ops:
  7.2 1.0 copy-start
  7.2 27.6 %all-gather.3.cloned.1.call-start = ((), (), s32[]{:S(2)}) async-start(), calls=%async_computation.2 | async-start | bytes 1310720 | tf_op jit(solution)/shard_map/all_gather | solution.py:55
  10.2 565.3 %reduce-scatter.3.cloned.1.call-start = ((), (), s32[]{:S(2)}) async-start(), calls=%async_computation.3 | async-start | bytes 17301504 | tf_op jit(solution)/shard_map/reduce_scatter | solution.py:62
  34.7 7.9 copy-start.2
  34.7 7.9 copy-start.5
  34.7 7.9 copy-start.6
  214.6 361.0 %copy-start.4 = (bf16[256,512]{1,0:T(8,128)(2,1)S(1)}, bf16[256,512]{1,0:T(8,128)(2,1)}, u32[]{:S(2)}) copy-start(bf16[256,512]{1,0:T(8,128)(2,1)} %param.17) | copy-start | bytes 786436
  214.6 550.9 %all-gather.5.cloned.1.call-start = ((), (), s32[]{:S(2)}) async-start(), calls=%async_computation.4 | async-start | bytes 8650752 | tf_op jit(solution)/shard_map/all_gather | solution.py:65
  577.8 378.0 %reduce-scatter.5.cloned.1.call-start = ((), (), s32[]{:S(2)}) async-start(), calls=%async_computation.5 | async-start | bytes 2621440 | tf_op jit(solution)/shard_map/reduce_scatter | solution.py:70
  765.8 190.0 %copy-start.3 = (bf16[256,512]{1,0:T(8,128)(2,1)S(1)}, bf16[256,512]{1,0:T(8,128)(2,1)}, u32[]{:S(2)}) copy-start(bf16[256,512]{1,0:T(8,128)(2,1)} %param.11) | copy-start | bytes 786436
  915.8 1.3 copy-start.1
  917.2 191.4 %all-reduce.2.cloned.1.call-start = ((), (), s32[]{:S(2)}) async-start(), calls=%async_computation.6 | async-start | bytes 2097152 | tf_op jit(solution)/shard_map/psum | solution.py:77
Sparse Core Ops, SparseCore 0:
  10.3 24.3 all-gather.2
  214.7 360.7 reduce-scatter.2
  577.9 187.5 all-gather.4
  917.3 38.4 reduce-scatter.4
  961.7 146.8 all-reduce.1
where the time goes:
time: 1120 us
  waiting for transfers between devices  744 us (66%)
  other arithmetic  192 us (17%)
  matrix products  91 us (8%)
  local copies, waits for them, and re-layouts  75 us (7%)
  between operations  14.5 us (1%)
    reduce_scatter x1, waiting for transfers between devices, per_device(): lax.psum_scatter(partial_value, ('col', 'rep'), scatter_dimension=0, tile...  361 us
    all_gather x1, waiting for transfers between devices, per_device(): grid_grads = lax.all_gather(grad_agg, ('col', 'rep'), axis=0, tiled=True)  188 us
    psum x1, waiting for transfers between devices, per_device(): grad_weight = lax.psum(weight_term, ('row', 'col', 'rep'))  148 us
    scatter-add x6, other arithmetic, aggregate_step(): return total.at[block_rows].add(prod)  113 us
    scatter-add x6, other arithmetic, spread_step(): return total.at[block_cols].add(prod)  70.6 us
    dot_general x6, matrix products, aggregate_step(): jnp.einsum('tij,tjf->tif', block_values, source[block_cols], preferred_el...  42.1 us
    dot_general x6, matrix products, spread_step(): jnp.einsum('tij,tif->tjf', block_values, source[block_rows], preferred_el...  41.9 us
    reduce_scatter x1, waiting for transfers between devices, per_device(): grad_proj = lax.psum_scatter(terms, 'row', scatter_dimension=0, tiled=True)  38.6 us
  transfers between devices with their start and end apart: 5, of which 5 were waited for; matrix products, arithmetic and copies ran while one was open for 2% of the time, Pallas kernels for 0%

commit v1 on v0

v1 whole, which is shorter than its diff:
```python
import math

import jax
import jax.numpy as jnp
from jax import lax
from jax.experimental import pallas as pl
from jax.experimental.pallas import tpu as pltpu
from jax.sharding import PartitionSpec as P

MESH = pl.DeviceIdType.MESH
F32, BF16 = jnp.float32, jnp.bfloat16
TILE = 128
NODES = 256
HALF = 256
WIDTH = 512
PEERS = 4
CHUNKS = 32
COLS = 1024
LOADS = 8
C0 = math.sqrt(2.0 / math.pi)


def place_kernel(rows, cols, count, values, dense, tiles, block, in_sem, out_sem):
    slots = tiles.shape[0]
    load = pltpu.make_async_copy(values, tiles, in_sem)
    load.start()

    def clear(i, carry):
        block[pl.ds(pl.multiple_of(i * 64, 64), 64), :] = jnp.zeros((64, COLS), BF16)
        return carry

    lax.fori_loop(0, block.shape[0] // 64, clear, 0)
    load.wait()

    def place(t, carry):
        row = pl.ds(pl.multiple_of(rows[t] * TILE, TILE), TILE)
        col = pl.ds(pl.multiple_of(cols[t] * TILE, TILE), TILE)
        block[row, col] = block[row, col] + tiles[t]
        return carry

    lax.fori_loop(0, jnp.minimum(count[0], slots), place, 0)
    store = pltpu.make_async_copy(block, dense, out_sem)
    store.start()
    store.wait()


def place_tiles(values, rows, cols, count):
    slots = values.shape[0]
    smem = pl.BlockSpec(memory_space=pltpu.SMEM)
    return pl.pallas_call(
        place_kernel,
        out_shape=jax.ShapeDtypeStruct((CHUNKS * NODES, COLS), BF16),
        in_specs=[smem, smem, smem, pl.BlockSpec(memory_space=pl.ANY)],
        out_specs=pl.BlockSpec(memory_space=pl.ANY),
        scratch_shapes=[
            pltpu.VMEM((slots, TILE, TILE), BF16),
            pltpu.VMEM((CHUNKS * NODES, COLS), BF16),
            pltpu.SemaphoreType.DMA,
            pltpu.SemaphoreType.DMA,
        ],
        compiler_params=pltpu.CompilerParams(vmem_limit_bytes=40 * 2**20),
        name="place_tiles",
    )(rows, cols, count, values)


def dot(a, b):
    return jnp.dot(a, b, preferred_element_type=F32)


def split(v):
    high = v.astype(BF16)
    return high, (v - high.astype(F32)).astype(BF16)


def layer_kernel(
    features, weight, dense_hbm, output_grad, output, grad_features, grad_weight,
    dense, feats, source, far_out, near_out, far_in, near_in, far2_out, near2_out, far2_in, near2_in,
    pair_out, pair_in, kept, grads, terms, col_out, col_in, col2_out, col2_in,
    wcore_out, wcore_in, wx, wx_out, wx_in, wz, wz_out, wz_in, wy, wy_out, wy_in, ygath, wfull,
    load_sem, a_s, a_r, far_s, far_r, near_s, near_r, far2_s, far2_r, near2_s, near2_r, pair_s, pair_r,
    g_s, g_r, c_s, c_r, c2_s, c2_r, wc_s, wc_r, wx_s, wx_r, wz_s, wz_r, wy_s, wy_r,
    gy_s, gy_r, gz_s, gz_r, gx_s, gx_r, gc_s, gc_r,
):
    row, z, rep = lax.axis_index("row"), lax.axis_index("col"), lax.axis_index("rep")
    high, core = row // 2, row % 2
    x, low = rep // 2, rep % 2

    def at(high_=None, core_=None, z_=None, x_=None, low_=None):
        pick = lambda v, own: own if v is None else v
        return {
            "row": pick(high_, high) * 2 + pick(core_, core),
            "col": pick(z_, z),
            "rep": pick(x_, x) * 2 + pick(low_, low),
        }

    def along(axis, step):
        return at(x_=(x + step) % 4) if axis == "x" else at(z_=(z + step) % 4)

    axes = (("x", "z"), ("z", "x"))
    spots = ((x, z), (z, x))

    def chunk(p, first, second, pair):
        if p == 0:
            return second * 8 + first * 2 + pair
        return first * 8 + second * 2 + pair

    def copy(src, dst, s, r, device):
        return pltpu.make_async_remote_copy(
            src_ref=src, dst_ref=dst, send_sem=s, recv_sem=r, device_id=device, device_id_type=MESH
        )

    cores, pair, across = at(core_=1 - core), at(low_=1 - low), at(high_=1 - high)
    ypeer = (pair, across, at(high_=1 - high, low_=1 - low))

    def loop(n, body):
        def step(i, carry):
            body(i)
            return carry

        lax.fori_loop(0, n, step, 0)

    per_load = CHUNKS * NODES // LOADS

    def load(i):
        span = pl.ds(pl.multiple_of(i * per_load, per_load), per_load)
        return pltpu.make_async_copy(dense_hbm.at[span], dense.at[span], load_sem.at[i])

    loop(LOADS, lambda i: load(i).start())

    barrier = pltpu.get_barrier_semaphore()
    partners = [along(axis, step) for axis in ("x", "z") for step in (1, 2, 3)] + list(ypeer) + [cores]
    for device in partners:
        pl.semaphore_signal(barrier, inc=1, device_id=device, device_id_type=MESH)
    pl.semaphore_wait(barrier, len(partners))

    row_across, row_core, row_last = (1 - high) * 2 + core, high * 2 + 1 - core, (1 - high) * 2 + 1 - core
    gather = (
        lambda r: copy(features, feats.at[r], a_s.at[0], a_r.at[0], across),
        lambda r: copy(features, feats.at[r], a_s.at[1], a_r.at[1], cores),
        lambda r: copy(feats.at[r], feats.at[r], a_s.at[2], a_r.at[2], cores),
    )
    gather[0](row).start()
    gather[1](row).start()
    feats[row] = features[...]

    def project(r):
        span = pl.ds(pl.multiple_of(r * NODES, NODES), NODES)
        source[span, :] = dot(feats[r], weight[...]).astype(BF16)

    project(row)
    gather[1](row_core).wait_recv()
    project(row_core)
    gather[0](row_across).wait_recv()
    gather[2](row_across).start()
    project(row_across)
    gather[2](row_last).wait_recv()
    project(row_last)
    loop(LOADS, lambda i: load(i).wait())

    def partial(p, first, second, pair_):
        start = pl.multiple_of(chunk(p, first, second, pair_) * NODES, NODES)
        return dot(dense[pl.ds(start, NODES), :], source[:, p * HALF:(p + 1) * HALF])

    steps = (3, 1)

    def far(p, o, d):
        return copy(far_out.at[p, o, d], far_in.at[p, o, d], far_s.at[p, o, d], far_r.at[p, o, d], along(axes[p][0], steps[d]))

    def near(p, o, d, y):
        return copy(
            near_out.at[p, o, d, y], near_in.at[p, o, d, y], near_s.at[p, o, d, y], near_r.at[p, o, d, y],
            along(axes[p][0], steps[d]),
        )

    def order(t):
        late = t // 2
        return (1 - late) * (2 - t) + late * 3 * (3 - t)

    def send_far(t):
        o = order(t)
        for p in range(2):
            first, second = spots[p]
            for d in range(2):
                far_out[p, o, d] = partial(p, (first + 2) % 4, (second + o) % 4, d).astype(BF16)
                far(p, o, d).start()

    def send_near(t):
        o = order(t)
        for p in range(2):
            first, second = spots[p]
            for d in range(2):
                near_out[p, o, d, 1 - d] = partial(p, (first + steps[d]) % 4, (second + o) % 4, 1 - d).astype(BF16)
                near(p, o, d, 1 - d).start()

    def send_added(t):
        o = order(t)
        for p in range(2):
            first, second = spots[p]
            for d in range(2):
                value = partial(p, (first + steps[d]) % 4, (second + o) % 4, d)
                far(p, o, d).wait_recv()
                near_out[p, o, d, d] = (value + far_in[p, o, d].astype(F32)).astype(BF16)
                near(p, o, d, d).start()

    loop(4, send_far)
    loop(4, send_near)
    loop(4, send_added)

    def far2(p, d):
        return copy(far2_out.at[p, d], far2_in.at[p, d], far2_s.at[p, d], far2_r.at[p, d], along(axes[p][1], steps[d]))

    def near2(p, d, y):
        return copy(
            near2_out.at[p, d, y], near2_in.at[p, d, y], near2_s.at[p, d, y], near2_r.at[p, d, y], along(axes[p][1], steps[d])
        )

    def first_sum(p, o, y):
        value = partial(p, spots[p][0], (spots[p][1] + o) % 4, y)
        near(p, o, 0, y).wait_recv()
        near(p, o, 1, y).wait_recv()
        return value + near_in[p, o, 0, y].astype(F32) + near_in[p, o, 1, y].astype(F32)

    for p in range(2):
        for d in range(2):
            far2_out[p, d] = first_sum(p, 2, d).astype(BF16)
            far2(p, d).start()
    for o, d in ((1, 1), (3, 0)):
        for p in range(2):
            near2_out[p, d, 1 - d] = first_sum(p, o, 1 - d).astype(BF16)
            near2(p, d, 1 - d).start()
            value = first_sum(p, o, d)
            far2(p, d).wait_recv()
            near2_out[p, d, d] = (value + far2_in[p, d].astype(F32)).astype(BF16)
            near2(p, d, d).start()
    for p in range(2):
        for y in range(2):
            kept[p, y] = first_sum(p, 0, y)

    def pairs(p):
        return copy(pair_out.at[p], pair_in.at[p], pair_s.at[p], pair_r.at[p], pair)

    for p in range(2):
        for y in range(2):
            for d in range(2):
                near2(p, d, y).wait_recv()
            kept[p, y] = kept[p, y] + near2_in[p, 0, y].astype(F32) + near2_in[p, 1, y].astype(F32)
        pair_out[p] = kept[p, 1 - low].astype(BF16)
        pairs(p).start()

    def slot(p, i, j, y):
        back = {1: 3, 3: 1}
        if i == 0:
            device = along(axes[p][1], 1 if (j == 3 or (j == 2 and y == 1)) else 3)
            src = grads.at[p, 0, 0, y] if j != 2 else grads.at[p, 0, 1 if y == 0 else 3, y]
        else:
            device = along(axes[p][0], 1 if (i == 3 or (i == 2 and y == 1)) else 3)
            src = grads.at[p, 0, j, y] if i != 2 else grads.at[p, 1 if y == 0 else 3, j, y]
        return copy(src, grads.at[p, i, j, y], g_s.at[p, i, j, y], g_r.at[p, i, j, y], device)

    def own_block(p, y):
        return copy(grads.at[p, 0, 0, y], grads.at[p, 0, 0, y], g_s.at[p, 0, 0, 0], g_r.at[p, 0, 0, 0], pair)

    for p in range(2):
        pairs(p).wait_recv()
        v = kept[p, low] + pair_in[p].astype(F32)
        span = slice(p * HALF, (p + 1) * HALF)
        t = jnp.tanh(C0 * (v + 0.044715 * (v * v * v)))
        output[:, span] = (0.5 * v * (1.0 + t)).astype(BF16)
        slope = 0.5 * (1.0 + t) + 0.5 * v * (1.0 - t * t) * (C0 * (1.0 + 3.0 * 0.044715 * (v * v)))
        grad = (output_grad[:, span].astype(F32) * slope).astype(BF16)
        grads[p, 0, 0, low] = grad.astype(F32).T.astype(BF16)
        own_block(p, low).start()

    for p in range(2):
        own_block(p, 1 - low).wait_recv()
        for j in (1, 3):
            for y in range(2):
                slot(p, 0, j, y).start()
        for i in (1, 3):
            for y in range(2):
                slot(p, i, 0, y).start()

    def product(p, i, j):
        first, second = spots[p]
        total = None
        for y in range(2):
            start = pl.multiple_of(chunk(p, (first + i) % 4, (second + j) % 4, y) * NODES, NODES)
            term = dot(grads[p, i, j, y], dense[pl.ds(start, NODES), :])
            total = term if total is None else total + term
        return total

    def add(p, i, j, fresh=False):
        total = product(p, i, j)
        for r in range(PEERS):
            part = total[:, r * NODES:(r + 1) * NODES]
            terms[p, r] = part if fresh else terms[p, r] + part

    for p in range(2):
        add(p, 0, 0, fresh=True)

    def arrive_first(j):
        for p in range(2):
            slot(p, 1, j, 0).wait_recv()
            slot(p, 2, j, 0).start()
            slot(p, 3, j, 1).wait_recv()
            slot(p, 2, j, 1).start()

    def use_first(j):
        for p in range(2):
            slot(p, 1, j, 1).wait_recv()
            add(p, 1, j)
            slot(p, 3, j, 0).wait_recv()
            add(p, 3, j)

    for p in range(2):
        slot(p, 0, 1, 0).wait_recv()
        slot(p, 0, 2, 0).start()
        slot(p, 0, 3, 1).wait_recv()
        slot(p, 0, 2, 1).start()
    for p in range(2):
        slot(p, 0, 1, 1).wait_recv()
        slot(p, 0, 3, 0).wait_recv()
        for j in (1, 3):
            for i in (1, 3):
                for y in range(2):
                    slot(p, i, j, y).start()
    arrive_first(0)
    for p in range(2):
        add(p, 0, 1)
        add(p, 0, 3)
    for p in range(2):
        for y in range(2):
            slot(p, 0, 2, y).wait_recv()
        for i in (1, 3):
            for y in range(2):
                slot(p, i, 2, y).start()
    for p in range(2):
        add(p, 0, 2)
    use_first(0)

    def middle(t):
        j = (1 - t // 2) * (2 * t + 1) + (t // 2) * 2
        arrive_first(j)
        use_first(j)

    loop(3, middle)

    def last(j):
        for p in range(2):
            for y in range(2):
                slot(p, 2, j, y).wait_recv()
            add(p, 2, j)

    loop(4, last)

    def cols1(h):
        return copy(col_out.at[h], col_in.at[h], c_s.at[h], c_r.at[h], cores)

    cols2 = copy(col2_out, col2_in, c2_s, c2_r, across)
    for h in range(2):
        for p in range(2):
            col_out[h, p] = terms[p, 2 * h + 1 - core].astype(BF16)
        cols1(h).start()

    def weight_half(p):
        total = jnp.zeros((HALF, WIDTH), F32)
        for r in range(PEERS):
            top, rest = split(terms[p, r])
            total = total + dot(top, feats[r]) + dot(rest, feats[r])
        return total

    weight_core = copy(wcore_out, wcore_in, wc_s, wc_r, cores)
    wcore_out[...] = weight_half(1 - core).astype(BF16)
    weight_core.start()
    wx[...] = weight_half(core).reshape(4, 64, WIDTH)
    weight_core.wait_recv()
    wx[...] = wx[...] + wcore_in[...].astype(F32).reshape(4, 64, WIDTH)

    def weight_x(s):
        return copy(wx_out.at[s], wx_in.at[s], wx_s.at[s], wx_r.at[s], along("x", s + 1))

    for s in range(3):
        wx_out[s] = wx[(x + s + 1) % 4].astype(BF16)
        weight_x(s).start()

    cols1(1 - high).wait_recv()
    for p in range(2):
        col2_out[p] = (terms[p, row_across] + col_in[1 - high, p].astype(F32)).astype(BF16)
    cols2.start()

    for s in range(3):
        weight_x(s).wait_recv()
    wz[...] = (
        wx[x] + wx_in[0].astype(F32) + wx_in[1].astype(F32) + wx_in[2].astype(F32)
    ).reshape(4, 16, WIDTH)

    def weight_z(s):
        return copy(wz_out.at[s], wz_in.at[s], wz_s.at[s], wz_r.at[s], along("z", s + 1))

    for s in range(3):
        wz_out[s] = wz[(z + s + 1) % 4]
        weight_z(s).start()
    cols1(high).wait_recv()
    for s in range(3):
        weight_z(s).wait_recv()
    total = wz[z] + wz_in[0] + wz_in[1] + wz_in[2]
    for s in range(4):
        wy[s] = total[:, s * TILE:(s + 1) * TILE]
    y = high * 2 + low
    yspot = (high * 2 + 1 - low, (1 - high) * 2 + low, (1 - high) * 2 + 1 - low)

    def weight_y(s):
        return copy(wy.at[yspot[s]], wy_in.at[s], wy_s.at[s], wy_r.at[s], ypeer[s])

    for s in range(3):
        weight_y(s).start()

    cols2.wait_recv()
    for p in range(2):
        value = terms[p, row] + col_in[high, p].astype(F32) + col2_in[p].astype(F32)
        kept[p, 0] = value.T
    contract = (((1,), (1,)), ((), ()))
    total = jnp.zeros((NODES, WIDTH), F32)
    for p in range(2):
        for part in split(kept[p, 0]):
            total = total + lax.dot_general(
                part, weight[:, p * HALF:(p + 1) * HALF], contract, preferred_element_type=F32
            )
    grad_features[...] = total.astype(BF16)

    for s in range(3):
        weight_y(s).wait_recv()
    ygath[y] = (wy[y] + wy_in[0] + wy_in[1] + wy_in[2]).astype(BF16)

    def gather_y(s, spot):
        return copy(ygath.at[spot], ygath.at[spot], gy_s.at[s], gy_r.at[s], ypeer[s])

    for s in range(3):
        gather_y(s, y).start()
    for s in range(3):
        gather_y(s, yspot[s]).wait_recv()
    for s in range(4):
        wfull[core, x, z, :, s * TILE:(s + 1) * TILE] = ygath[s]

    def gather_z(s, spot):
        return copy(wfull.at[core, x, spot], wfull.at[core, x, spot], gz_s.at[s], gz_r.at[s], along("z", s + 1))

    for s in range(3):
        gather_z(s, z).start()
    for s in range(3):
        gather_z(s, (z + 3 - s) % 4).wait_recv()

    def gather_x(s, spot):
        return copy(wfull.at[core, spot], wfull.at[core, spot], gx_s.at[s], gx_r.at[s], along("x", s + 1))

    for s in range(3):
        gather_x(s, x).start()
    for s in range(3):
        gather_x(s, (x + 3 - s) % 4).wait_recv()

    def gather_core(spot):
        return copy(wfull.at[spot], wfull.at[spot], gc_s, gc_r, cores)

    gather_core(core).start()
    gather_core(1 - core).wait_recv()
    grad_weight[...] = wfull[...].reshape(WIDTH, WIDTH).astype(F32)

    gather[0](row).wait_send()
    gather[1](row).wait_send()
    gather[2](row_across).wait_send()

    def sent(o):
        for p in range(2):
            for d in range(2):
                far(p, o, d).wait_send()
                for y in range(2):
                    near(p, o, d, y).wait_send()

    loop(4, sent)
    for p in range(2):
        for d in range(2):
            far2(p, d).wait_send()
            for y in range(2):
                near2(p, d, y).wait_send()
        pairs(p).wait_send()
        own_block(p, low).wait_send()
        for j in (1, 2, 3):
            for y in range(2):
                slot(p, 0, j, y).wait_send()

    def sent_grads(j):
        for p in range(2):
            for i in (1, 2, 3):
                for y in range(2):
                    slot(p, i, j, y).wait_send()

    loop(4, sent_grads)
    for h in range(2):
        cols1(h).wait_send()
    cols2.wait_send()
    weight_core.wait_send()
    for s in range(3):
        weight_x(s).wait_send()
        weight_z(s).wait_send()
        weight_y(s).wait_send()
        gather_y(s, y).wait_send()
        gather_z(s, z).wait_send()
        gather_x(s, x).wait_send()
    gather_core(core).wait_send()


def layer(features, weight, dense, output_grad):
    vmem = pl.BlockSpec(memory_space=pltpu.VMEM)
    dma = pltpu.SemaphoreType.DMA
    block = (NODES, HALF)
    bf = lambda *shape: pltpu.VMEM(shape, BF16)
    f32 = lambda *shape: pltpu.VMEM(shape, F32)
    return pl.pallas_call(
        layer_kernel,
        out_shape=(
            jax.ShapeDtypeStruct((NODES, WIDTH), BF16),
            jax.ShapeDtypeStruct((NODES, WIDTH), BF16),
            jax.ShapeDtypeStruct((WIDTH, WIDTH), F32),
        ),
        in_specs=[vmem, vmem, pl.BlockSpec(memory_space=pl.ANY), vmem],
        out_specs=(vmem, vmem, vmem),
        scratch_shapes=[
            bf(CHUNKS * NODES, COLS),
            bf(PEERS, NODES, WIDTH),
            bf(COLS, WIDTH),
            bf(2, 4, 2, *block),
            bf(2, 4, 2, 2, *block),
            bf(2, 4, 2, *block),
            bf(2, 4, 2, 2, *block),
            bf(2, 2, *block),
            bf(2, 2, 2, *block),
            bf(2, 2, *block),
            bf(2, 2, 2, *block),
            bf(2, *block),
            bf(2, *block),
            f32(2, 2, *block),
            bf(2, 4, 4, 2, HALF, NODES),
            f32(2, PEERS, HALF, NODES),
            bf(2, 2, HALF, NODES),
            bf(2, 2, HALF, NODES),
            bf(2, HALF, NODES),
            bf(2, HALF, NODES),
            bf(HALF, WIDTH),
            bf(HALF, WIDTH),
            f32(4, 64, WIDTH),
            bf(3, 64, WIDTH),
            bf(3, 64, WIDTH),
            f32(4, 16, WIDTH),
            f32(3, 16, WIDTH),
            f32(3, 16, WIDTH),
            f32(4, 16, TILE),
            f32(3, 16, TILE),
            f32(3, 16, TILE),
            bf(4, 16, TILE),
            bf(2, 4, 4, 16, WIDTH),
            dma((LOADS,)),
            dma((3,)), dma((3,)),
            dma((2, 4, 2)), dma((2, 4, 2)),
            dma((2, 4, 2, 2)), dma((2, 4, 2, 2)),
            dma((2, 2)), dma((2, 2)),
            dma((2, 2, 2)), dma((2, 2, 2)),
            dma((2,)), dma((2,)),
            dma((2, 4, 4, 2)), dma((2, 4, 4, 2)),
            dma((2,)), dma((2,)),
            dma, dma,
            dma, dma,
            dma((3,)), dma((3,)),
            dma((3,)), dma((3,)),
            dma((3,)), dma((3,)),
            dma((3,)), dma((3,)),
            dma((3,)), dma((3,)),
            dma((3,)), dma((3,)),
            dma, dma,
        ],
        compiler_params=pltpu.CompilerParams(
            collective_id=0, has_side_effects=True, vmem_limit_bytes=60 * 2**20
        ),
        name="layer",
    )(features, weight, dense, output_grad)


def per_device(features, weight, tile_values, tile_rows, tile_cols, tile_count, output_grad):
    dense = place_tiles(tile_values, tile_rows, tile_cols, tile_count)
    output, grad_features, grad_weight = layer(features, weight, dense, output_grad)
    return output, grad_features, grad_weight.T


def solution(mesh):
    spread = P(("row", "col", "rep"))
    return jax.shard_map(
        per_device,
        mesh=mesh,
        in_specs=(
            P(("row", "col", "rep"), None),
            P(),
            P(("row", "col", "rep"), None, None),
            spread,
            spread,
            spread,
            P(("row", "col", "rep"), None),
        ),
        out_specs=(P(("row", "col", "rep"), None), P(("row", "col", "rep"), None), P()),
        check_vma=False,
    )
```

time: 1120 us -> 180 us (0.16)
  waiting for transfers between devices: 744 us -> 0 us
  other arithmetic: 192 us -> 0 us
  Pallas kernels: 0 us -> 169 us
  matrix products: 91 us -> 0 us
  local copies, waits for them, and re-layouts: 75 us -> 10 us
  between operations: 14.5 us -> 1.31 us
    reduce_scatter x2 -> x0, waiting for transfers between devices: 399 us -> none  [the longest x1 361 us: per_device(): lax.psum_scatter(partial_value, ('col', 'rep'), scatter_dimension=0, tile...]
    all_gather x2 -> x0, waiting for transfers between devices: 197 us -> none  [the longest x1 188 us: per_device(): grid_grads = lax.all_gather(grad_agg, ('col', 'rep'), axis=0, tiled=True)]
    scatter-add x12 -> x0, other arithmetic: 183 us -> none  [the longest x6 113 us: aggregate_step(): return total.at[block_rows].add(prod)]
    pallas_call x0 -> x2, Pallas kernels: none -> 169 us  [the longest x1 160 us: layer(): pl.pallas_call(layer_kernel, out_shape=(jax.ShapeDtypeStruct((NODES, WIDT...]
    psum x1 -> x0, waiting for transfers between devices: 148 us -> none  [per_device(): grad_weight = lax.psum(weight_term, ('row', 'col', 'rep'))]
    dot_general x15 -> x0, matrix products: 91 us -> none  [the longest x6 42.1 us: aggregate_step(): jnp.einsum('tij,tjf->tif', block_values, source[block_cols], preferred_el...]
    gather x12 -> x0, local copies, waits for them, and re-layouts: 53.5 us -> none  [the longest x6 36.8 us: spread_step(): source[block_rows]]
  transfers between devices with their start and end apart: 5 -> 0, of which waited for: 5 -> 0; matrix products, arithmetic and copies ran while one was open for 2% -> 0% of each run, Pallas kernels for 0% -> 0%
where the time goes in v1:
time: 180 us
  Pallas kernels  169 us (94%)
  local copies, waits for them, and re-layouts  10 us (6%)
    pallas_call x1, Pallas kernels, layer(): pl.pallas_call(layer_kernel, out_shape=(jax.ShapeDtypeStruct((NODES, WIDT...  160 us
    unnamed x9, local copies, waits for them, and re-layouts  10 us
    pallas_call x1, Pallas kernels, place_tiles(): pl.pallas_call(place_kernel, out_shape=jax.ShapeDtypeStruct((CHUNKS * NOD...  9.1 us

profile of v1, /device:TPU:1, one launch (start us, length us, event | category | flops | bytes accessed | tf_op | source)
XLA Modules:
  0.0 180.0 jit_solution(10540668719275274184)
XLA Ops:
  1.3 0.0 copy-start
  1.3 2.8 %copy-done = bf16[192,128,128]{2,1,0:T(8,128)(2,1)S(1)} copy-done((bf16[192,128,128]{2,1,0:T(8,128)(2,1)S(1)}, bf16[192,128,128]{2,1,0:T(8,128)(2,1)}, u32[]{:S(2)}) %copy-start) | copy-done | bytes 6291480
  4.1 0.0 copy-start.1
  4.1 0.7 copy-done.1
  4.7 0.0 copy-start.2
  4.7 0.7 copy-done.2
  5.4 9.1 %place_tiles.1.dense_hbm = bf16[8192,1024]{1,0:T(8,128)(2,1)} custom-call(s32[192]{0:T(256)S(1)} %copy-done.1, s32[192]{0:T(256)S(1)} %copy-done.2, s32[1]{0:T(128)S(6)} %copy.13.count, bf16[192,128,128]{2,1,0:T(8,128)(2,1)S(1)} %copy-done), custom_call_target="tpu_custom_call" | custom-call | tf_op jit(solution)/shard_map/place_tiles/pallas_call | solution.py:50
  14.5 159.6 %layer.1 = (bf16[256,512]{1,0:T(8,128)(2,1)}, bf16[256,512]{1,0:T(8,128)(2,1)}, f32[512,512]{1,0:T(8,128)}) custom-call(bf16[256,512]{1,0:T(8,128)(2,1)} %features.1, bf16[512,512]{1,0:T(8,128)(2,1)} %weight.1, bf16[8192,1024]{1,0:T(8,128)(2,1)} %place_tiles.1.dense_hbm, bf16[256,512]{1,0:T(8,128)(2,1)} %output_grad.1), custom_call_target="tpu_custom_call" | custom-call | tf_op jit(solution)/shard_map/layer/pallas_call | solution.py:518
  174.2 2.5 %copy.10 = f32[512,512]{1,0:T(8,128)} copy(f32[512,512]{0,1:T(8,128)} %bitcast.1) | data formatting | bytes 2097152
  176.7 1.7 copy.14
  178.4 1.7 copy.15
Async XLA Ops:
  1.3 2.8 %copy-start = (bf16[192,128,128]{2,1,0:T(8,128)(2,1)S(1)}, bf16[192,128,128]{2,1,0:T(8,128)(2,1)}, u32[]{:S(2)}) copy-start(bf16[192,128,128]{2,1,0:T(8,128)(2,1)} %values.1) | copy-start | bytes 18874372
  4.1 0.7 copy-start.1
  4.7 0.7 copy-start.2

commit v2 on v0

v2 whole, which is shorter than its diff:
```python
import math

import jax
import jax.numpy as jnp
from jax import lax
from jax.experimental import pallas as pl
from jax.experimental.pallas import tpu as pltpu
from jax.sharding import PartitionSpec as P

MESH = pl.DeviceIdType.MESH
F32, BF16 = jnp.float32, jnp.bfloat16
TILE = 128
NODES = 256
HALF = 256
WIDTH = 512
PEERS = 4
CHUNKS = 32
COLS = 1024
LOADS = 8
C0 = math.sqrt(2.0 / math.pi)


def place_kernel(rows, cols, count, values, dense, tiles, block, in_sem, out_sem):
    slots = tiles.shape[0]
    load = pltpu.make_async_copy(values, tiles, in_sem)
    load.start()

    def clear(i, carry):
        block[pl.ds(pl.multiple_of(i * 64, 64), 64), :] = jnp.zeros((64, COLS), BF16)
        return carry

    lax.fori_loop(0, block.shape[0] // 64, clear, 0)
    load.wait()

    def place(t, carry):
        row = pl.ds(pl.multiple_of(rows[t] * TILE, TILE), TILE)
        col = pl.ds(pl.multiple_of(cols[t] * TILE, TILE), TILE)
        block[row, col] = block[row, col] + tiles[t]
        return carry

    lax.fori_loop(0, jnp.minimum(count[0], slots), place, 0)
    store = pltpu.make_async_copy(block, dense, out_sem)
    store.start()
    store.wait()


def place_tiles(values, rows, cols, count):
    slots = values.shape[0]
    smem = pl.BlockSpec(memory_space=pltpu.SMEM)
    return pl.pallas_call(
        place_kernel,
        out_shape=jax.ShapeDtypeStruct((CHUNKS * NODES, COLS), BF16),
        in_specs=[smem, smem, smem, pl.BlockSpec(memory_space=pl.ANY)],
        out_specs=pl.BlockSpec(memory_space=pl.ANY),
        scratch_shapes=[
            pltpu.VMEM((slots, TILE, TILE), BF16),
            pltpu.VMEM((CHUNKS * NODES, COLS), BF16),
            pltpu.SemaphoreType.DMA,
            pltpu.SemaphoreType.DMA,
        ],
        cost_estimate=pl.CostEstimate(flops=0, bytes_accessed=30 * 2**20, transcendentals=0),
        compiler_params=pltpu.CompilerParams(vmem_limit_bytes=63 * 2**20),
        name="place_tiles",
    )(rows, cols, count, values)


def dot(a, b):
    return jnp.dot(a, b, preferred_element_type=F32)


def split(v):
    high = v.astype(BF16)
    return high, (v - high.astype(F32)).astype(BF16)


def layer_kernel(
    features, features_across, weight_hbm, dense_hbm, output_grad_hbm, output_hbm, grad_features_hbm, grad_weight_hbm,
    dense, feats, weight, output_grad, output, grad_features, lifted,
    pairs_out, pairs_in, far_out, far_in, near_out, near_in, far2_out, far2_in, near2_out, near2_in, pair_out, pair_in,
    kept, grads, terms, col_out, col_in, col2_out, col2_in,
    wcore_out, wcore_in, wsum, wy_out, wy_in, wgrid, wgrid_in, ggrid, wfull,
    load_sem, in_sem, out_sem, a_s, a_r, pairs_s, pairs_r, far_s, far_r, near_s, near_r, far2_s, far2_r, near2_s, near2_r,
    pair_s, pair_r, g_s, own_r, second_r, first_r, gfar_r, gpair_r, c_s, c_r, c2_s, c2_r, w_s, w_r,
):
    row, z, rep = lax.axis_index("row"), lax.axis_index("col"), lax.axis_index("rep")
    high, core = row // 2, row % 2
    x, low = rep // 2, rep % 2

    def at(high_=None, core_=None, z_=None, x_=None, low_=None):
        pick = lambda v, own: own if v is None else v
        return {
            "row": pick(high_, high) * 2 + pick(core_, core),
            "col": pick(z_, z),
            "rep": pick(x_, x) * 2 + pick(low_, low),
        }

    def along(axis, step):
        return at(x_=(x + step) % 4) if axis == "x" else at(z_=(z + step) % 4)

    def on_grid(s):
        return at(x_=(x + s // 4) % 4, z_=(z + s % 4) % 4)

    axes = (("x", "z"), ("z", "x"))
    spots = ((x, z), (z, x))
    steps = (3, 1)
    mine, other = low, 1 - low

    def chunk(p, first, second, pair_):
        if p == 0:
            return second * 8 + first * 2 + pair_
        return first * 8 + second * 2 + pair_

    def copy(src, dst, s, r, device):
        return pltpu.make_async_remote_copy(
            src_ref=src, dst_ref=dst, send_sem=s, recv_sem=r, device_id=device, device_id_type=MESH
        )

    cores, pair, across = at(core_=1 - core), at(low_=1 - low), at(high_=1 - high)
    ypeer = (pair, across, at(high_=1 - high, low_=1 - low))

    def loop(n, body):
        def step(i, carry):
            body(i)
            return carry

        lax.fori_loop(0, n, step, 0)

    def rows_of(r):
        return pl.ds(pl.multiple_of(r * NODES, NODES), NODES)

    per_load = CHUNKS * NODES // LOADS

    def load(i):
        span = pl.ds(pl.multiple_of(i * per_load, per_load), per_load)
        return pltpu.make_async_copy(dense_hbm.at[span], dense.at[span], load_sem.at[i])

    row_across, row_core, row_last = (1 - high) * 2 + core, high * 2 + 1 - core, (1 - high) * 2 + 1 - core
    takes = (
        pltpu.make_async_copy(features, feats.at[rows_of(row)], in_sem.at[0]),
        pltpu.make_async_copy(features_across, feats.at[rows_of(row_across)], in_sem.at[1]),
        pltpu.make_async_copy(weight_hbm, weight, in_sem.at[2]),
        pltpu.make_async_copy(output_grad_hbm, output_grad, in_sem.at[3]),
    )
    takes[0].start()
    takes[1].start()
    loop(LOADS, lambda i: load(i).start())
    takes[2].start()
    takes[3].start()

    barrier = pltpu.get_barrier_semaphore()

    def greet(s):
        pl.semaphore_signal(barrier, inc=1, device_id=on_grid(s + 1), device_id_type=MESH)

    loop(15, greet)
    for device in (*ypeer, cores):
        pl.semaphore_signal(barrier, inc=1, device_id=device, device_id_type=MESH)
    pl.semaphore_wait(barrier, 19)

    def gather(i, r):
        return copy((features, features_across)[i], feats.at[rows_of(r)], a_s.at[i], a_r.at[i], cores)

    gather(0, row).start()
    gather(1, row_across).start()
    takes[0].wait()
    takes[1].wait()
    gather(0, row_core).wait_recv()
    gather(1, row_last).wait_recv()
    loop(LOADS, lambda i: load(i).wait())

    def partial(p, first, second, pair_):
        start = pl.multiple_of(chunk(p, first, second, pair_) * NODES, NODES)
        return dot(dense[pl.ds(start, NODES), :], feats[:, p * HALF:(p + 1) * HALF])

    def pairs(p, o):
        return copy(pairs_out.at[p, o], pairs_in.at[p, o], pairs_s, pairs_r.at[p, o], pair)

    def far(p, o, d):
        half = pl.ds(d * TILE, TILE)
        return copy(far_out.at[p, o, half], far_in.at[p, o, d], far_s, far_r.at[p, o, d], along(axes[p][0], steps[d]))

    def near(p, o, r, d):
        return copy(near_out.at[p, o, r, d], near_in.at[p, o, r, d], near_s, near_r.at[p, o, r], along(axes[p][0], steps[d]))

    def near_both(p, o, r):
        return copy(near_out.at[p, o, r], near_in.at[p, o, r], near_s, near_r.at[p, o, r], pair)

    def send_other(o):
        for p in range(2):
            first, second = spots[p]
            for d in range(2):
                near_out[p, o, 1, d] = partial(p, (first + steps[d]) % 4, (second + o) % 4, other).astype(BF16)
                near(p, o, 1, d).start()

    def send_pair(o):
        for p in range(2):
            first, second = spots[p]
            pairs_out[p, o] = partial(p, (first + 2) % 4, (second + o) % 4, other).astype(BF16)
            pairs(p, o).start()

    def send_far(o):
        for p in range(2):
            first, second = spots[p]
            value = partial(p, (first + 2) % 4, (second + o) % 4, mine)
            pairs(p, o).wait_recv()
            far_out[p, o] = (value + pairs_in[p, o].astype(F32)).astype(BF16)
            for d in range(2):
                far(p, o, d).start()

    def send_mine(o):
        for p in range(2):
            first, second = spots[p]
            for d in range(2):
                value = partial(p, (first + steps[d]) % 4, (second + o) % 4, mine)
                far(p, o, d).wait_recv()
                half, rest = (slice(0, TILE), slice(TILE, NODES))[::1 - 2 * d]
                near_out[p, o, 0, d, half] = (value[half] + far_in[p, o, d].astype(F32)).astype(BF16)
                near_out[p, o, 0, d, rest] = value[rest].astype(BF16)
                near(p, o, 0, d).start()

    def far2(p, d):
        return copy(far2_out.at[p, d], far2_in.at[p, d], far2_s, far2_r.at[p, d], along(axes[p][1], 3 - 2 * d))

    def near2(p, d, y):
        return copy(near2_out.at[p, y, d], near2_in.at[p, y, d], near2_s, near2_r.at[p, y], along(axes[p][1], 3 - 2 * d))

    def near2_both(p, y):
        return copy(near2_out.at[p, y], near2_in.at[p, y], near2_s, near2_r.at[p, y], pair)

    def first_sum(p, o, y):
        value = partial(p, spots[p][0], (spots[p][1] + o) % 4, y)
        r = (y + low) % 2
        near_both(p, o, r).wait_recv()
        return value + near_in[p, o, r, 0].astype(F32) + near_in[p, o, r, 1].astype(F32)

    def send_far2(d):
        for p in range(2):
            far2_out[p, d] = first_sum(p, 2, d).astype(BF16)
            far2(p, d).start()

    def send_other2(d):
        for p in range(2):
            near2_out[p, 1 - d, d] = first_sum(p, 3 - 2 * d, 1 - d).astype(BF16)
            near2(p, d, 1 - d).start()

    def send_mine2(d):
        for p in range(2):
            value = first_sum(p, 3 - 2 * d, d)
            far2(p, d).wait_recv()
            near2_out[p, d, d] = (value + far2_in[p, d].astype(F32)).astype(BF16)
            near2(p, d, d).start()

    def keep(y):
        for p in range(2):
            kept[p, y] = first_sum(p, 0, y)

    def last_pair(p):
        return copy(pair_out.at[p], pair_in.at[p], pair_s, pair_r.at[p], pair)

    def second_sum(p, y):
        near2_both(p, y).wait_recv()
        return kept[p, y] + near2_in[p, y, 0].astype(F32) + near2_in[p, y, 1].astype(F32)

    def send_last():
        for p in range(2):
            pair_out[p] = second_sum(p, other).astype(BF16)
            last_pair(p).start()

    def keep_last():
        for p in range(2):
            kept[p, mine] = second_sum(p, mine)

    for step in (
        (send_other, 0), (send_pair, 2), (send_other, 2), (send_other, 1), (send_pair, 1), (send_far, 2),
        (send_other, 3), (send_pair, 3), (send_mine, 2), (keep, other), (send_far2, other), (send_pair, 0),
        (send_far, 1), (send_other2, mine), (send_far, 3), (send_far2, mine), (send_mine2, other), (send_mine, 1),
        (send_far, 0), (send_mine, 3), (send_mine, 0), (send_last,), (send_other2, other), (send_mine2, mine),
        (keep, mine), (keep_last,),
    ):
        step[0](*step[1:])

    takes[2].wait()
    takes[3].wait()
    v = jnp.zeros((NODES, WIDTH), F32)
    for p in range(2):
        last_pair(p).wait_recv()
        span = slice(p * HALF, (p + 1) * HALF)
        for i, part in enumerate(split(kept[p, mine] + pair_in[p].astype(F32))):
            lifted[i, :, span] = part
            v = v + dot(part, weight[span, :])
    t = jnp.tanh(C0 * (v + 0.044715 * (v * v * v)))
    slope = 0.5 * (1.0 + t) + 0.5 * v * (1.0 - t * t) * (C0 * (1.0 + 3.0 * 0.044715 * (v * v)))
    grad = (output_grad[...].astype(F32) * slope).astype(BF16).astype(F32)

    def own(p, y):
        return copy(grads.at[p, 0, 0, y], grads.at[p, 0, 0, y], g_s.at[0], own_r.at[p], pair)

    def second(p, j, y):
        step, src = {1: (3, 0), 2: (3 - 2 * y, 1 + 2 * y), 3: (1, 0)}[j]
        return copy(
            grads.at[p, 0, src, y], grads.at[p, 0, j, y], g_s.at[2 if j == 2 else 1], second_r.at[p, j - 1, y],
            along(axes[p][1], step),
        )

    def first(p, i, j, y):
        return copy(
            grads.at[p, 0, j, y], grads.at[p, i, j, y], g_s.at[3], first_r.at[p, i // 2, j, y],
            along(axes[p][0], 3 if i == 1 else 1),
        )

    def onward(p, j, d):
        half = pl.ds(d * TILE, TILE)
        return copy(
            grads.at[p, 1 + 2 * d, j, mine, half], grads.at[p, 2, j, mine, half], g_s.at[4], gfar_r.at[p, j],
            along(axes[p][0], steps[d]),
        )

    def onward_both(p, j):
        return copy(grads.at[p, 2, j, mine], grads.at[p, 2, j, mine], g_s.at[4], gfar_r.at[p, j], pair)

    def far_pair(p, j, y):
        return copy(grads.at[p, 2, j, y], grads.at[p, 2, j, y], g_s.at[5], gpair_r.at[p, j], pair)

    def give_first(p, j, y):
        first(p, 1, j, y).start()
        first(p, 3, j, y).start()

    def give_second(p, y):
        second(p, 1, y).start()
        second(p, 3, y).start()

    for p in range(2):
        grads[p, 0, 0, mine] = grad[:, p * HALF:(p + 1) * HALF].T.astype(BF16)
        give_second(p, mine)
    output[...] = (0.5 * v * (1.0 + t)).astype(BF16)
    gives = (
        pltpu.make_async_copy(output, output_hbm, out_sem.at[0]),
        pltpu.make_async_copy(wfull, grad_weight_hbm, out_sem.at[1]),
        pltpu.make_async_copy(grad_features, grad_features_hbm, out_sem.at[2]),
    )
    gives[0].start()

    def weight_half(p):
        block = grads[p, 0, 0, mine]
        return dot(block, lifted[0]) + dot(block, lifted[1])

    spot = x * 4 + z
    y = high * 2 + low
    yspot = (high * 2 + other, (1 - high) * 2 + low, (1 - high) * 2 + other)
    weight_core = copy(wcore_out, wcore_in, w_s.at[0], w_r.at[0], cores)

    def weight_y(s):
        return copy(wy_out.at[s], wy_in.at[s], w_s.at[1], w_r.at[1], ypeer[s])

    def weight_grid(s):
        part = ((x + s // 4) % 4) * 4 + (z + s % 4) % 4
        return copy(wgrid.at[part], wgrid_in.at[s], w_s.at[2], w_r.at[2], on_grid(s))

    def gather_grid(s):
        return copy(ggrid.at[spot], ggrid.at[spot], w_s.at[3], w_r.at[3], on_grid(s))

    def gather_y(s):
        return copy(wfull.at[core, y], wfull.at[core, y], w_s.at[4], w_r.at[4], ypeer[s])

    def gather_core(half):
        return copy(wfull.at[half], wfull.at[half], w_s.at[5], w_r.at[5], cores)

    weight_all = (
        weight_core,
        copy(wy_out, wy_in, w_s.at[1], w_r.at[1], cores),
        copy(wgrid.at[pl.ds(1, 15)], wgrid_in.at[pl.ds(1, 15)], w_s.at[2], w_r.at[2], cores),
        copy(ggrid.at[pl.ds(1, 15)], ggrid.at[pl.ds(1, 15)], w_s.at[3], w_r.at[3], cores),
        copy(wfull.at[0, pl.ds(0, 3)], wfull.at[0, pl.ds(0, 3)], w_s.at[4], w_r.at[4], cores),
        gather_core(1 - core),
    )

    def weight_step(k):
        if k > 0:
            weight_all[k - 1].wait_recv()
        if k == 0:
            wcore_out[...] = weight_half(1 - core).astype(BF16)
            weight_core.start()
            wsum[...] = weight_half(core).reshape(4, 64, WIDTH)
        elif k == 1:
            wsum[...] = wsum[...] + wcore_in[...].astype(F32).reshape(4, 64, WIDTH)
            for s in range(3):
                wy_out[s] = wsum[yspot[s]].astype(BF16)
                weight_y(s).start()
        elif k == 2:
            total = wsum[y]
            for s in range(3):
                total = total + wy_in[s].astype(F32)
            for s in range(16):
                i, j = s // 4, s % 4
                wgrid[s] = total[i * 16:(i + 1) * 16, j * TILE:(j + 1) * TILE]
            loop(15, lambda s: weight_grid(s + 1).start())
        elif k == 3:
            total = wgrid[spot]
            for s in range(1, 16):
                total = total + wgrid_in[s]
            ggrid[spot] = total.astype(BF16)
            loop(15, lambda s: gather_grid(s + 1).start())
        elif k == 4:
            for s in range(16):
                i, j = s // 4, s % 4
                wfull[core, y, i * 16:(i + 1) * 16, j * TILE:(j + 1) * TILE] = ggrid[s]
            for s in range(3):
                gather_y(s).start()
        elif k == 5:
            gather_core(core).start()
        else:
            gives[1].start()

    def product(p, i, j):
        total = None
        for y_ in range(2):
            start = chunk(p, (spots[p][0] + i) % 4, (spots[p][1] + j) % 4, y_) * NODES
            term = dot(grads[p, i, j, y_], dense[pl.ds(pl.multiple_of(start, NODES), NODES), :])
            total = term if total is None else total + term
        return total

    begun = set()

    def add(p, i, j):
        total, fresh = product(p, i, j), p not in begun
        begun.add(p)
        for r in range(PEERS):
            part = total[:, r * NODES:(r + 1) * NODES]
            terms[p, r] = part if fresh else terms[p, r] + part

    def pass_on(j):
        for p in range(2):
            for d in range(2):
                first(p, 1 + 2 * d, j, mine).wait_recv()
                onward(p, j, d).start()

    def pass_pair(j):
        for p in range(2):
            onward_both(p, j).wait_recv()
            far_pair(p, j, mine).start()

    def use_first(j):
        for p in range(2):
            for i in (1, 3):
                first(p, i, j, other).wait_recv()
                add(p, i, j)

    def use_far(j):
        for p in range(2):
            far_pair(p, j, other).wait_recv()
            add(p, 2, j)

    def give_own():
        for p in range(2):
            own(p, mine).start()

    def take_own():
        for p in range(2):
            own(p, other).wait_recv()
            give_second(p, other)

    def give_firsts(j, y_):
        for p in range(2):
            give_first(p, j, y_)

    def take_second(y_):
        for p in range(2):
            second(p, 1, y_).wait_recv()
            second(p, 3, y_).wait_recv()
            second(p, 2, y_).start()

    def take_second2(y_):
        for p in range(2):
            second(p, 2, y_).wait_recv()

    def use_own(j):
        for p in range(2):
            add(p, 0, j)

    for step in (
        (weight_step, 0), (give_firsts, 0, mine), (give_own,), (take_second, mine), (give_firsts, 3, mine), (pass_on, 0),
        (take_own,), (weight_step, 1), (take_second2, mine), (give_firsts, 2, mine), (pass_on, 3), (weight_step, 2),
        (pass_pair, 0), (give_firsts, 1, mine), (take_second, other), (pass_on, 2), (use_own, 3), (pass_pair, 3),
        (give_firsts, 0, other), (use_own, 1), (weight_step, 3), (pass_on, 1), (pass_pair, 2), (take_second2, other),
        (use_own, 0), (give_firsts, 1, other), (give_firsts, 3, other), (pass_pair, 1), (give_firsts, 2, other),
        (use_first, 0), (use_far, 2), (use_first, 1), (weight_step, 4), (use_far, 3), (use_far, 0), (use_own, 2),
        (use_first, 3), (use_far, 1), (use_first, 2),
    ):
        step[0](*step[1:])

    def cols1(h):
        return copy(col_out.at[h], col_in.at[h], c_s, c_r.at[h], cores)

    cols2 = copy(col2_out, col2_in, c2_s, c2_r, across)

    def give_cols(h):
        for p in range(2):
            col_out[h, p] = terms[p, 2 * h + 1 - core].astype(BF16)
        cols1(h).start()

    give_cols(1 - high)
    give_cols(high)
    cols1(1 - high).wait_recv()
    for p in range(2):
        col2_out[p] = (terms[p, row_across] + col_in[1 - high, p].astype(F32)).astype(BF16)
    cols2.start()
    weight_step(5)
    weight_step(6)

    def sent(ref, sem):
        copy(ref, ref, sem, sem, pair).wait_send()

    for i, r in ((0, row), (1, row_across)):
        gather(i, r).wait_send()
    sent(pairs_out, pairs_s)
    sent(far_out, far_s)
    sent(near_out, near_s)
    sent(far2_out, far2_s)
    sent(near2_out, near2_s)
    sent(pair_out, pair_s)
    sent(grads.at[0, 0, 0], g_s.at[0])
    sent(grads.at[0, 0], g_s.at[1])
    sent(grads.at[0, 0, pl.ds(0, 2)], g_s.at[2])
    sent(grads.at[0], g_s.at[3])
    sent(grads.at[0, 0], g_s.at[4])
    sent(grads.at[0, 0], g_s.at[5])
    for step in weight_all:
        step.wait_send()
    gives[0].wait()
    gives[1].wait()

    cols1(high).wait_recv()
    cols2.wait_recv()
    contract = (((1,), (1,)), ((), ()))
    total = jnp.zeros((NODES, WIDTH), F32)
    for p in range(2):
        value = (terms[p, row] + col_in[high, p].astype(F32) + col2_in[p].astype(F32)).T
        for part in split(value):
            total = total + lax.dot_general(
                part, weight[:, p * HALF:(p + 1) * HALF], contract, preferred_element_type=F32
            )
    grad_features[...] = total.astype(BF16)
    gives[2].start()
    sent(col_out, c_s)
    cols2.wait_send()
    gives[2].wait()


def layer(features, features_across, weight, dense, output_grad):
    anywhere = pl.BlockSpec(memory_space=pl.ANY)
    dma = pltpu.SemaphoreType.DMA
    block = (NODES, HALF)
    bf = lambda *shape: pltpu.VMEM(shape, BF16)
    f32 = lambda *shape: pltpu.VMEM(shape, F32)
    return pl.pallas_call(
        layer_kernel,
        out_shape=(
            jax.ShapeDtypeStruct((NODES, WIDTH), BF16),
            jax.ShapeDtypeStruct((NODES, WIDTH), BF16),
            jax.ShapeDtypeStruct((2, 4, 64, WIDTH), BF16),
        ),
        in_specs=[anywhere] * 5,
        out_specs=(anywhere,) * 3,
        scratch_shapes=[
            bf(CHUNKS * NODES, COLS),
            bf(COLS, WIDTH),
            bf(WIDTH, WIDTH),
            bf(NODES, WIDTH),
            bf(NODES, WIDTH),
            bf(NODES, WIDTH),
            bf(2, NODES, WIDTH),
            bf(2, 4, *block), bf(2, 4, *block),
            bf(2, 4, *block), bf(2, 4, 2, TILE, HALF),
            bf(2, 4, 2, 2, *block), bf(2, 4, 2, 2, *block),
            bf(2, 2, *block), bf(2, 2, *block),
            bf(2, 2, 2, *block), bf(2, 2, 2, *block),
            bf(2, *block), bf(2, *block),
            f32(2, 2, *block),
            bf(2, 4, 4, 2, HALF, NODES),
            f32(2, PEERS, HALF, NODES),
            bf(2, 2, HALF, NODES), bf(2, 2, HALF, NODES),
            bf(2, HALF, NODES), bf(2, HALF, NODES),
            bf(HALF, WIDTH), bf(HALF, WIDTH),
            f32(4, 64, WIDTH),
            bf(3, 64, WIDTH), bf(3, 64, WIDTH),
            f32(16, 16, TILE), f32(16, 16, TILE),
            bf(16, 16, TILE),
            bf(2, 4, 64, WIDTH),
            dma((LOADS,)), dma((4,)), dma((3,)),
            dma((2,)), dma((2,)),
            dma, dma((2, 4)),
            dma, dma((2, 4, 2)),
            dma, dma((2, 4, 2)),
            dma, dma((2, 2)),
            dma, dma((2, 2)),
            dma, dma((2,)),
            dma((6,)), dma((2,)), dma((2, 3, 2)), dma((2, 2, 4, 2)), dma((2, 4)), dma((2, 4)),
            dma, dma((2,)),
            dma, dma,
            dma((6,)), dma((6,)),
        ],
        compiler_params=pltpu.CompilerParams(
            collective_id=0, has_side_effects=True, vmem_limit_bytes=62 * 2**20
        ),
        name="layer",
    )(features, features_across, weight, dense, output_grad)


def finish_kernel(first_in, second_in, weight_in, first, second, weight):
    first[...] = first_in[...]
    second[...] = second_in[...]
    weight[...] = weight_in[...].astype(F32).T


def finish(output, grad_features, grad_weight):
    vmem = pl.BlockSpec(memory_space=pltpu.VMEM)
    return pl.pallas_call(
        finish_kernel,
        out_shape=(
            jax.ShapeDtypeStruct(output.shape, BF16),
            jax.ShapeDtypeStruct(grad_features.shape, BF16),
            jax.ShapeDtypeStruct(grad_weight.shape, F32),
        ),
        in_specs=[vmem] * 3,
        out_specs=(vmem,) * 3,
        compiler_params=pltpu.CompilerParams(vmem_limit_bytes=63 * 2**20),
        name="finish",
    )(output, grad_features, grad_weight)


def per_device(features, weight, tile_values, tile_rows, tile_cols, tile_count, output_grad):
    features_across = lax.ppermute(features, "row", [(r, (r + 2) % PEERS) for r in range(PEERS)])
    dense = place_tiles(tile_values, tile_rows, tile_cols, tile_count)
    output, grad_features, grad_weight = layer(features, features_across, weight, dense, output_grad)
    return finish(output, grad_features, grad_weight.reshape(WIDTH, WIDTH))


def solution(mesh):
    spread = P(("row", "col", "rep"))
    return jax.shard_map(
        per_device,
        mesh=mesh,
        in_specs=(
            P(("row", "col", "rep"), None),
            P(),
            P(("row", "col", "rep"), None, None),
            spread,
            spread,
            spread,
            P(("row", "col", "rep"), None),
        ),
        out_specs=(P(("row", "col", "rep"), None), P(("row", "col", "rep"), None), P()),
        check_vma=False,
    )
```

time: 1120 us -> 128 us (0.11)
  waiting for transfers between devices: 744 us -> 0.01 us
  other arithmetic: 192 us -> 0 us
  Pallas kernels: 0 us -> 122 us
  matrix products: 91 us -> 0 us
  local copies, waits for them, and re-layouts: 75 us -> 0.7 us
  between operations: 14.5 us -> 1.32 us
    reduce_scatter x2 -> x0, waiting for transfers between devices: 399 us -> none  [the longest x1 361 us: per_device(): lax.psum_scatter(partial_value, ('col', 'rep'), scatter_dimension=0, tile...]
    all_gather x2 -> x0, waiting for transfers between devices: 197 us -> none  [the longest x1 188 us: per_device(): grid_grads = lax.all_gather(grad_agg, ('col', 'rep'), axis=0, tiled=True)]
    scatter-add x12 -> x0, other arithmetic: 183 us -> none  [the longest x6 113 us: aggregate_step(): return total.at[block_rows].add(prod)]
    psum x1 -> x0, waiting for transfers between devices: 148 us -> none  [per_device(): grad_weight = lax.psum(weight_term, ('row', 'col', 'rep'))]
    pallas_call x0 -> x3, Pallas kernels: none -> 122 us  [the longest x1 108 us: layer(): pl.pallas_call(layer_kernel, out_shape=(jax.ShapeDtypeStruct((NODES, WIDT...]
    dot_general x15 -> x0, matrix products: 91 us -> none  [the longest x6 42.1 us: aggregate_step(): jnp.einsum('tij,tjf->tif', block_values, source[block_cols], preferred_el...]
    gather x12 -> x0, local copies, waits for them, and re-layouts: 53.5 us -> none  [the longest x6 36.8 us: spread_step(): source[block_rows]]
    unnamed x16 -> x2, local copies, waits for them, and re-layouts: 13.4 us -> 0.7 us
  transfers between devices with their start and end apart: 5 -> 1, of which waited for: 5 -> 0; matrix products, arithmetic and copies ran while one was open for 2% -> 0% of each run, Pallas kernels for 0% -> 9%
where the time goes in v2:
time: 128 us
  Pallas kernels  122 us (95%)
  starting transfers between devices  3.82 us (3%)
  between operations  1.32 us (1%)
    pallas_call x1, Pallas kernels, layer(): pl.pallas_call(layer_kernel, out_shape=(jax.ShapeDtypeStruct((NODES, WIDT...  108 us
    pallas_call x1, Pallas kernels, place_tiles(): pl.pallas_call(place_kernel, out_shape=jax.ShapeDtypeStruct((CHUNKS * NOD...  11.4 us
    ppermute x1, starting transfers between devices, per_device(): lax.ppermute(features, 'row', [(r, (r + 2) % PEERS) for r in range(PEERS)])  3.82 us
  transfers between devices with their start and end apart: 1, of which 0 were waited for; matrix products, arithmetic and copies ran while one was open for 0% of the time, Pallas kernels for 9%

profile of v2, /device:TPU:1, one launch (start us, length us, event | category | flops | bytes accessed | tf_op | source)
XLA Modules:
  0.0 127.7 jit_solution(18253636587063009511)
XLA Ops:
  0.6 3.8 %collective-permute-start = (bf16[256,512]{1,0:T(8,128)(2,1)}, bf16[256,512]{1,0:T(8,128)(2,1)S(1)}, u32[]{:S(2)}, u32[]{:S(2)}) collective-permute-start(bf16[256,512]{1,0:T(8,128)(2,1)} %features.1), channel_id=1, source_target_pairs={{0,64},{32,96},{64,0},{96,32},{1,65},{33,97},{65,1},{97,33},{2,66}... | collective-permute-start | bytes 786440 | tf_op jit(solution)/shard_map/ppermute | solution.py:632
  5.1 11.4 %place_tiles.1.dense_hbm = bf16[8192,1024]{1,0:T(8,128)(2,1)} custom-call(s32[192]{0:T(256)} %rows.1, s32[192]{0:T(256)} %cols.1, s32[1]{0:T(128)S(6)} %copy.10.count, bf16[192,128,128]{2,1,0:T(8,128)(2,1)} %values.1), custom_call_target="tpu_custom_call" | custom-call | bytes 31457280 | tf_op jit(solution)/shard_map/place_tiles/pallas_call | solution.py:50
  16.5 0.0 collective-permute-done.features_across
  16.5 0.0 copy-start
  16.6 0.7 copy-done
  17.2 107.9 %layer.1 = (bf16[256,512]{1,0:T(8,128)(2,1)}, bf16[256,512]{1,0:T(8,128)(2,1)}, bf16[2,4,64,512]{3,2,1,0:T(8,128)(2,1)}) custom-call(bf16[256,512]{1,0:T(8,128)(2,1)} %features.1, bf16[256,512]{1,0:T(8,128)(2,1)} %copy-done, bf16[512,512]{1,0:T(8,128)(2,1)} %weight_hbm.1, bf16[8192,1024]{1,0:T(8,128)(2,1)} %place_tiles.1.dense_hbm, ...), custom_call_target="tpu_custom_call" | custom-call | tf_op jit(solution)/shard_map/layer/pallas_call | solution.py:555
  125.1 2.5 %finish.1 = (bf16[256,512]{1,0:T(8,128)(2,1)}, bf16[256,512]{1,0:T(8,128)(2,1)}, f32[512,512]{1,0:T(8,128)}) custom-call(bf16[256,512]{1,0:T(8,128)(2,1)} %get-tuple-element.6.first_in, bf16[256,512]{1,0:T(8,128)(2,1)} %get-tuple-element.7.second_in, bf16[512,512]{1,0:T(8,128)(2,1)} %bitcast.1), custom_call_target="tpu_custom_call" | custom-call | tf_op jit(solution)/shard_map/finish/pallas_call | solution.py:617
Async XLA Ops:
  0.6 15.9 %collective-permute-start = (bf16[256,512]{1,0:T(8,128)(2,1)}, bf16[256,512]{1,0:T(8,128)(2,1)S(1)}, u32[]{:S(2)}, u32[]{:S(2)}) collective-permute-start(bf16[256,512]{1,0:T(8,128)(2,1)} %features.1), channel_id=1, source_target_pairs={{0,64},{32,96},{64,0},{96,32},{1,65},{33,97},{65,1},{97,33},{2,66}... | collective-permute-start | bytes 786440 | tf_op jit(solution)/shard_map/ppermute | solution.py:632
  16.5 0.7 copy-start

commit v3 on v2

--- a/solution.py
+++ b/solution.py
@@ -16,15 +16,29 @@
 PEERS = 4
 CHUNKS = 32
 COLS = 1024
-LOADS = 8
+BANDS = 8
+BAND_TILES = 8
+PLACE_VMEM, LAYER_VMEM, FINISH_VMEM = 63 * 2**20, 62 * 2**20, 63 * 2**20
 C0 = math.sqrt(2.0 / math.pi)
 
 
-def place_kernel(rows, cols, count, values, dense, tiles, block, in_sem, out_sem):
+def place_kernel(rows, cols, count, values, dense, tiles, block, listed, filled, in_sem, out_sem):
     slots = tiles.shape[0]
     load = pltpu.make_async_copy(values, tiles, in_sem)
     load.start()
 
+    for g in range(BANDS):
+        filled[g] = 0
+
+    def enlist(t, carry):
+        g = rows[t] // BAND_TILES
+        at = filled[g]
+        listed[g, at] = t
+        filled[g] = at + 1
+        return carry
+
+    lax.fori_loop(0, jnp.minimum(count[0], slots), enlist, 0)
+
     def clear(i, carry):
         block[pl.ds(pl.multiple_of(i * 64, 64), 64), :] = jnp.zeros((64, COLS), BF16)
         return carry
@@ -32,16 +46,22 @@
     lax.fori_loop(0, block.shape[0] // 64, clear, 0)
     load.wait()
 
-    def place(t, carry):
-        row = pl.ds(pl.multiple_of(rows[t] * TILE, TILE), TILE)
-        col = pl.ds(pl.multiple_of(cols[t] * TILE, TILE), TILE)
-        block[row, col] = block[row, col] + tiles[t]
-        return carry
-
-    lax.fori_loop(0, jnp.minimum(count[0], slots), place, 0)
-    store = pltpu.make_async_copy(block, dense, out_sem)
-    store.start()
-    store.wait()
+    def store(g):
+        band = pl.ds(pl.multiple_of(g * BAND_TILES * TILE, BAND_TILES * TILE), BAND_TILES * TILE)
+        return pltpu.make_async_copy(block.at[band], dense.at[band], out_sem.at[g])
+
+    for g in range(BANDS):
+        def place(i, carry):
+            t = listed[g, i]
+            row = pl.ds(pl.multiple_of(rows[t] * TILE, TILE), TILE)
+            col = pl.ds(pl.multiple_of(cols[t] * TILE, TILE), TILE)
+            block[row, col] = block[row, col] + tiles[t]
+            return carry
+
+        lax.fori_loop(0, filled[g], place, 0)
+        store(g).start()
+    for g in range(BANDS):
+        store(g).wait()
 
 
 def place_tiles(values, rows, cols, count):
@@ -55,11 +75,13 @@
         scratch_shapes=[
             pltpu.VMEM((slots, TILE, TILE), BF16),
             pltpu.VMEM((CHUNKS * NODES, COLS), BF16),
+            pltpu.SMEM((BANDS, slots), jnp.int32),
+            pltpu.SMEM((BANDS,), jnp.int32),
             pltpu.SemaphoreType.DMA,
-            pltpu.SemaphoreType.DMA,
+            pltpu.SemaphoreType.DMA((BANDS,)),
         ],
         cost_estimate=pl.CostEstimate(flops=0, bytes_accessed=30 * 2**20, transcendentals=0),
-        compiler_params=pltpu.CompilerParams(vmem_limit_bytes=63 * 2**20),
+        compiler_params=pltpu.CompilerParams(vmem_limit_bytes=PLACE_VMEM),
         name="place_tiles",
     )(rows, cols, count, values)
 
@@ -78,7 +100,7 @@
     dense, feats, weight, output_grad, output, grad_features, lifted,
     pairs_out, pairs_in, far_out, far_in, near_out, near_in, far2_out, far2_in, near2_out, near2_in, pair_out, pair_in,
     kept, grads, terms, col_out, col_in, col2_out, col2_in,
-    wcore_out, wcore_in, wsum, wy_out, wy_in, wgrid, wgrid_in, ggrid, wfull,
+    wcore_out, wcore_in, wsum, wy_in, wgrid, wgrid_in, ggrid, wfull,
     load_sem, in_sem, out_sem, a_s, a_r, pairs_s, pairs_r, far_s, far_r, near_s, near_r, far2_s, far2_r, near2_s, near2_r,
     pair_s, pair_r, g_s, own_r, second_r, first_r, gfar_r, gpair_r, c_s, c_r, c2_s, c2_r, w_s, w_r,
 ):
@@ -128,11 +150,32 @@
     def rows_of(r):
         return pl.ds(pl.multiple_of(r * NODES, NODES), NODES)
 
-    per_load = CHUNKS * NODES // LOADS
-
-    def load(i):
-        span = pl.ds(pl.multiple_of(i * per_load, per_load), per_load)
-        return pltpu.make_async_copy(dense_hbm.at[span], dense.at[span], load_sem.at[i])
+    def load(i, j, pair_):
+        span = rows_of(chunk(0, (x + i) % 4, (z + j) % 4, pair_))
+        sem = load_sem.at[i, j, 0 if pair_ is mine else 1]
+        return pltpu.make_async_copy(dense_hbm.at[span], dense.at[span], sem)
+
+    uses = [(steps[d], o, other) for o in (0,) for d in range(2)]
+    uses += [(2, 2, other)] + [(steps[d], 2, other) for d in range(2)] + [(steps[d], 1, other) for d in range(2)]
+    uses += [(2, 1, other), (2, 2, mine)] + [(steps[d], 3, other) for d in range(2)] + [(2, 3, other)]
+    uses += [(steps[d], 2, mine) for d in range(2)]
+    waiting = []
+    for i, j, pair_ in uses + [(i, j, pair_) for pair_ in (other, mine) for i in range(4) for j in range(4)]:
+        for key in ((i, j, pair_), (j, i, pair_)):
+            if not any(key[:2] == k[:2] and key[2] is k[2] for k in waiting):
+                waiting.append(key)
+    loads = list(waiting)
+
+    def need(p, i, j, pair_):
+        for key in waiting:
+            if key[:2] == ((i, j), (j, i))[p] and key[2] is pair_:
+                load(*key).wait()
+                waiting.remove(key)
+                break
+
+    def need_all():
+        while waiting:
+            load(*waiting.pop(0)).wait()
 
     row_across, row_core, row_last = (1 - high) * 2 + core, high * 2 + 1 - core, (1 - high) * 2 + 1 - core
     takes = (
@@ -143,9 +186,8 @@
     )
     takes[0].start()
     takes[1].start()
-    loop(LOADS, lambda i: load(i).start())
-    takes[2].start()
-    takes[3].start()
+    for key in loads[:2]:
+        load(*key).start()
 
     barrier = pltpu.get_barrier_semaphore()
 
@@ -164,9 +206,18 @@
     gather(1, row_across).start()
     takes[0].wait()
     takes[1].wait()
+    for key in loads[2:6]:
+        load(*key).start()
     gather(0, row_core).wait_recv()
     gather(1, row_last).wait_recv()
-    loop(LOADS, lambda i: load(i).wait())
+    for key in loads[6:]:
+        load(*key).start()
+    takes[2].start()
+    takes[3].start()
+
+    def partial_at(p, i, j, pair_):
+        need(p, i, j, pair_)
+        return partial(p, (spots[p][0] + i) % 4, (spots[p][1] + j) % 4, pair_)
 
     def partial(p, first, second, pair_):
         start = pl.multiple_of(chunk(p, first, second, pair_) * NODES, NODES)
@@ -185,38 +236,30 @@
     def near_both(p, o, r):
         return copy(near_out.at[p, o, r], near_in.at[p, o, r], near_s, near_r.at[p, o, r], pair)
 
-    def send_other(o):
-        for p in range(2):
-            first, second = spots[p]
-            for d in range(2):
-                near_out[p, o, 1, d] = partial(p, (first + steps[d]) % 4, (second + o) % 4, other).astype(BF16)
-                near(p, o, 1, d).start()
-
-    def send_pair(o):
-        for p in range(2):
-            first, second = spots[p]
-            pairs_out[p, o] = partial(p, (first + 2) % 4, (second + o) % 4, other).astype(BF16)
-            pairs(p, o).start()
-
-    def send_far(o):
-        for p in range(2):
-            first, second = spots[p]
-            value = partial(p, (first + 2) % 4, (second + o) % 4, mine)
-            pairs(p, o).wait_recv()
-            far_out[p, o] = (value + pairs_in[p, o].astype(F32)).astype(BF16)
-            for d in range(2):
-                far(p, o, d).start()
-
-    def send_mine(o):
-        for p in range(2):
-            first, second = spots[p]
-            for d in range(2):
-                value = partial(p, (first + steps[d]) % 4, (second + o) % 4, mine)
-                far(p, o, d).wait_recv()
-                half, rest = (slice(0, TILE), slice(TILE, NODES))[::1 - 2 * d]
-                near_out[p, o, 0, d, half] = (value[half] + far_in[p, o, d].astype(F32)).astype(BF16)
-                near_out[p, o, 0, d, rest] = value[rest].astype(BF16)
-                near(p, o, 0, d).start()
+    def send_other(p, o):
+        for d in range(2):
+            near_out[p, o, 1, d] = partial_at(p, steps[d], o, other).astype(BF16)
+            near(p, o, 1, d).start()
+
+    def send_pair(p, o):
+        pairs_out[p, o] = partial_at(p, 2, o, other).astype(BF16)
+        pairs(p, o).start()
+
+    def send_far(p, o):
+        value = partial_at(p, 2, o, mine)
+        pairs(p, o).wait_recv()
+        far_out[p, o] = (value + pairs_in[p, o].astype(F32)).astype(BF16)
+        for d in range(2):
+            far(p, o, d).start()
+
+    def send_mine(p, o):
+        for d in range(2):
+            value = partial_at(p, steps[d], o, mine)
+            far(p, o, d).wait_recv()
+            half, rest = (slice(0, TILE), slice(TILE, NODES))[::1 - 2 * d]
+            near_out[p, o, 0, d, half] = (value[half] + far_in[p, o, d].astype(F32)).astype(BF16)
+            near_out[p, o, 0, d, rest] = value[rest].astype(BF16)
+            near(p, o, 0, d).start()
 
     def far2(p, d):
         return copy(far2_out.at[p, d], far2_in.at[p, d], far2_s, far2_r.at[p, d], along(axes[p][1], 3 - 2 * d))
@@ -228,31 +271,28 @@
         return copy(near2_out.at[p, y], near2_in.at[p, y], near2_s, near2_r.at[p, y], pair)
 
     def first_sum(p, o, y):
+        need_all()
         value = partial(p, spots[p][0], (spots[p][1] + o) % 4, y)
         r = (y + low) % 2
         near_both(p, o, r).wait_recv()
         return value + near_in[p, o, r, 0].astype(F32) + near_in[p, o, r, 1].astype(F32)
 
-    def send_far2(d):
-        for p in range(2):
-            far2_out[p, d] = first_sum(p, 2, d).astype(BF16)
-            far2(p, d).start()
-
-    def send_other2(d):
-        for p in range(2):
-            near2_out[p, 1 - d, d] = first_sum(p, 3 - 2 * d, 1 - d).astype(BF16)
-            near2(p, d, 1 - d).start()
-
-    def send_mine2(d):
-        for p in range(2):
-            value = first_sum(p, 3 - 2 * d, d)
-            far2(p, d).wait_recv()
-            near2_out[p, d, d] = (value + far2_in[p, d].astype(F32)).astype(BF16)
-            near2(p, d, d).start()
-
-    def keep(y):
-        for p in range(2):
-            kept[p, y] = first_sum(p, 0, y)
+    def send_far2(p, d):
+        far2_out[p, d] = first_sum(p, 2, d).astype(BF16)
+        far2(p, d).start()
+
+    def send_other2(p, d):
+        near2_out[p, 1 - d, d] = first_sum(p, 3 - 2 * d, 1 - d).astype(BF16)
+        near2(p, d, 1 - d).start()
+
+    def send_mine2(p, d):
+        value = first_sum(p, 3 - 2 * d, d)
+        far2(p, d).wait_recv()
+        near2_out[p, d, d] = (value + far2_in[p, d].astype(F32)).astype(BF16)
+        near2(p, d, d).start()
+
+    def keep(p, y):
+        kept[p, y] = first_sum(p, 0, y)
 
     def last_pair(p):
         return copy(pair_out.at[p], pair_in.at[p], pair_s, pair_r.at[p], pair)
@@ -261,23 +301,21 @@
         near2_both(p, y).wait_recv()
         return kept[p, y] + near2_in[p, y, 0].astype(F32) + near2_in[p, y, 1].astype(F32)
 
-    def send_last():
+    def send_last(p):
+        pair_out[p] = second_sum(p, other).astype(BF16)
+        last_pair(p).start()
+
+    def keep_last(p):
+        kept[p, mine] = second_sum(p, mine)
+
+    for step in (
+        (send_other, 0), (send_pair, 2), (send_other, 2), (send_other, 1), (send_pair, 1), (send_far, 2), (send_other, 3),
+        (send_pair, 3), (send_mine, 2), (keep, other), (send_far2, other), (send_pair, 0), (send_far, 1), (send_other2, mine),
+        (send_far, 3), (send_far2, mine), (send_mine2, other), (send_mine, 1), (send_far, 0), (send_mine, 3), (send_mine, 0),
+        (send_last,), (send_other2, other), (send_mine2, mine), (keep, mine), (keep_last,),
+    ):
         for p in range(2):
-            pair_out[p] = second_sum(p, other).astype(BF16)
-            last_pair(p).start()
-
-    def keep_last():
-        for p in range(2):
-            kept[p, mine] = second_sum(p, mine)
-
-    for step in (
-        (send_other, 0), (send_pair, 2), (send_other, 2), (send_other, 1), (send_pair, 1), (send_far, 2),
-        (send_other, 3), (send_pair, 3), (send_mine, 2), (keep, other), (send_far2, other), (send_pair, 0),
-        (send_far, 1), (send_other2, mine), (send_far, 3), (send_far2, mine), (send_mine2, other), (send_mine, 1),
-        (send_far, 0), (send_mine, 3), (send_mine, 0), (send_last,), (send_other2, other), (send_mine2, mine),
-        (keep, mine), (keep_last,),
-    ):
-        step[0](*step[1:])
+            step[0](p, *step[1:])
 
     takes[2].wait()
     takes[3].wait()
@@ -331,15 +369,6 @@
 
     for p in range(2):
         grads[p, 0, 0, mine] = grad[:, p * HALF:(p + 1) * HALF].T.astype(BF16)
-        give_second(p, mine)
-    output[...] = (0.5 * v * (1.0 + t)).astype(BF16)
-    gives = (
-        pltpu.make_async_copy(output, output_hbm, out_sem.at[0]),
-        pltpu.make_async_copy(wfull, grad_weight_hbm, out_sem.at[1]),
-        pltpu.make_async_copy(grad_features, grad_features_hbm, out_sem.at[2]),
-    )
-    gives[0].start()
-
     def weight_half(p):
         block = grads[p, 0, 0, mine]
         return dot(block, lifted[0]) + dot(block, lifted[1])
@@ -350,7 +379,7 @@
     weight_core = copy(wcore_out, wcore_in, w_s.at[0], w_r.at[0], cores)
 
     def weight_y(s):
-        return copy(wy_out.at[s], wy_in.at[s], w_s.at[1], w_r.at[1], ypeer[s])
+        return copy(wsum.at[yspot[s]], wy_in.at[s], w_s.at[1], w_r.at[1], ypeer[s])
 
     def weight_grid(s):
         part = ((x + s // 4) % 4) * 4 + (z + s % 4) % 4
@@ -367,7 +396,7 @@
 
     weight_all = (
         weight_core,
-        copy(wy_out, wy_in, w_s.at[1], w_r.at[1], cores),
+        copy(wsum.at[pl.ds(0, 3)], wy_in, w_s.at[1], w_r.at[1], cores),
         copy(wgrid.at[pl.ds(1, 15)], wgrid_in.at[pl.ds(1, 15)], w_s.at[2], w_r.at[2], cores),
         copy(ggrid.at[pl.ds(1, 15)], ggrid.at[pl.ds(1, 15)], w_s.at[3], w_r.at[3], cores),
         copy(wfull.at[0, pl.ds(0, 3)], wfull.at[0, pl.ds(0, 3)], w_s.at[4], w_r.at[4], cores),
@@ -378,18 +407,17 @@
         if k > 0:
             weight_all[k - 1].wait_recv()
         if k == 0:
-            wcore_out[...] = weight_half(1 - core).astype(BF16)
+            wcore_out[...] = weight_half(1 - core)
             weight_core.start()
             wsum[...] = weight_half(core).reshape(4, 64, WIDTH)
         elif k == 1:
-            wsum[...] = wsum[...] + wcore_in[...].astype(F32).reshape(4, 64, WIDTH)
+            wsum[...] = wsum[...] + wcore_in[...].reshape(4, 64, WIDTH)
             for s in range(3):
-                wy_out[s] = wsum[yspot[s]].astype(BF16)
                 weight_y(s).start()
         elif k == 2:
             total = wsum[y]
             for s in range(3):
-                total = total + wy_in[s].astype(F32)
+                total = total + wy_in[s]
             for s in range(16):
                 i, j = s // 4, s % 4
                 wgrid[s] = total[i * 16:(i + 1) * 16, j * TILE:(j + 1) * TILE]
@@ -428,84 +456,90 @@
             part = total[:, r * NODES:(r + 1) * NODES]
             terms[p, r] = part if fresh else terms[p, r] + part
 
-    def pass_on(j):
-        for p in range(2):
-            for d in range(2):
-                first(p, 1 + 2 * d, j, mine).wait_recv()
-                onward(p, j, d).start()
-
-    def pass_pair(j):
-        for p in range(2):
-            onward_both(p, j).wait_recv()
-            far_pair(p, j, mine).start()
-
-    def use_first(j):
-        for p in range(2):
-            for i in (1, 3):
-                first(p, i, j, other).wait_recv()
-                add(p, i, j)
-
-    def use_far(j):
-        for p in range(2):
-            far_pair(p, j, other).wait_recv()
-            add(p, 2, j)
+    def pass_on(p, j):
+        for d in range(2):
+            first(p, 1 + 2 * d, j, mine).wait_recv()
+            onward(p, j, d).start()
+
+    def pass_pair(p, j):
+        onward_both(p, j).wait_recv()
+        far_pair(p, j, mine).start()
+
+    def use_first(p, j):
+        for i in (1, 3):
+            first(p, i, j, other).wait_recv()
+            add(p, i, j)
+
+    def use_far(p, j):
+        far_pair(p, j, other).wait_recv()
+        add(p, 2, j)
+
+    gives = (
+        pltpu.make_async_copy(output, output_hbm, out_sem.at[0]),
+        pltpu.make_async_copy(wfull, grad_weight_hbm, out_sem.at[1]),
+        pltpu.make_async_copy(grad_features, grad_features_hbm, out_sem.at[2]),
+    )
+
+    def give_output():
+        output[...] = (0.5 * v * (1.0 + t)).astype(BF16)
+        gives[0].start()
 
     def give_own():
         for p in range(2):
             own(p, mine).start()
 
-    def take_own():
-        for p in range(2):
-            own(p, other).wait_recv()
-            give_second(p, other)
-
-    def give_firsts(j, y_):
-        for p in range(2):
-            give_first(p, j, y_)
-
-    def take_second(y_):
-        for p in range(2):
-            second(p, 1, y_).wait_recv()
-            second(p, 3, y_).wait_recv()
-            second(p, 2, y_).start()
-
-    def take_second2(y_):
-        for p in range(2):
-            second(p, 2, y_).wait_recv()
-
-    def use_own(j):
-        for p in range(2):
-            add(p, 0, j)
+    def take_own(p):
+        own(p, other).wait_recv()
+
+    def give_firsts(p, j, y_):
+        give_first(p, j, y_)
+
+    def take_second(p, y_):
+        second(p, 1, y_).wait_recv()
+        second(p, 3, y_).wait_recv()
+        second(p, 2, y_).start()
+
+    def take_second2(p, y_):
+        second(p, 2, y_).wait_recv()
+
+    def use_own(p, j):
+        add(p, 0, j)
+
+    def cols1(p, h):
+        return copy(col_out.at[p, h], col_in.at[p, h], c_s, c_r.at[p, h], cores)
+
+    def cols2(p):
+        return copy(col2_out.at[p], col2_in.at[p], c2_s, c2_r.at[p], across)
+
+    def give_cols(p):
+        for h in (1 - high, high):
+            col_out[p, h] = terms[p, 2 * h + 1 - core].astype(BF16)
+            cols1(p, h).start()
+
+    def pass_cols(p):
+        cols1(p, 1 - high).wait_recv()
+        col2_out[p] = (terms[p, row_across] + col_in[p, 1 - high].astype(F32)).astype(BF16)
+        cols2(p).start()
 
     for step in (
-        (weight_step, 0), (give_firsts, 0, mine), (give_own,), (take_second, mine), (give_firsts, 3, mine), (pass_on, 0),
-        (take_own,), (weight_step, 1), (take_second2, mine), (give_firsts, 2, mine), (pass_on, 3), (weight_step, 2),
-        (pass_pair, 0), (give_firsts, 1, mine), (take_second, other), (pass_on, 2), (use_own, 3), (pass_pair, 3),
-        (give_firsts, 0, other), (use_own, 1), (weight_step, 3), (pass_on, 1), (pass_pair, 2), (take_second2, other),
-        (use_own, 0), (give_firsts, 1, other), (give_firsts, 3, other), (pass_pair, 1), (give_firsts, 2, other),
-        (use_first, 0), (use_far, 2), (use_first, 1), (weight_step, 4), (use_far, 3), (use_far, 0), (use_own, 2),
-        (use_first, 3), (use_far, 1), (use_first, 2),
+        (give_second, 0, mine), (give_second, 1, mine), (give_firsts, 1, 0, mine), (give_own,), (give_output,), (weight_step, 0),
+        (give_firsts, 0, 0, mine), (take_own, 0), (take_second, 1, mine), (give_firsts, 1, 3, mine), (take_own, 1),
+        (give_second, 1, other), (pass_on, 1, 0), (use_own, 0, 0), (pass_on, 0, 0), (give_second, 0, other),
+        (give_firsts, 1, 1, mine), (take_second, 0, mine), (take_second2, 1, mine), (weight_step, 1),
+        (give_firsts, 1, 2, mine), (pass_on, 1, 3), (give_firsts, 0, 1, mine), (pass_pair, 1, 0), (take_second, 1, other),
+        (take_second, 0, other), (use_own, 1, 1), (use_own, 0, 1), (give_firsts, 0, 3, mine), (take_second2, 1, other),
+        (pass_on, 0, 1), (pass_pair, 0, 0), (use_own, 1, 3), (take_second2, 0, mine), (pass_on, 0, 3), (weight_step, 2),
+        (pass_on, 1, 1), (pass_pair, 0, 1), (give_firsts, 0, 2, mine), (pass_pair, 0, 3), (give_firsts, 1, 2, other),
+        (pass_on, 1, 2), (pass_pair, 1, 3), (take_second2, 0, other), (pass_pair, 1, 1), (give_firsts, 0, 1, other),
+        (give_firsts, 0, 3, other), (weight_step, 3), (use_own, 0, 3), (give_firsts, 1, 1, other), (pass_pair, 1, 2),
+        (use_far, 1, 0), (give_firsts, 1, 3, other), (pass_on, 0, 2), (use_far, 0, 0), (use_far, 1, 3),
+        (give_firsts, 0, 0, other), (give_firsts, 0, 2, other), (use_own, 1, 0), (use_first, 0, 1), (use_far, 0, 3),
+        (give_firsts, 1, 0, other), (use_far, 0, 1), (use_far, 1, 1), (use_first, 1, 1), (pass_pair, 0, 2), (use_first, 1, 2),
+        (use_first, 0, 3), (use_first, 1, 3), (weight_step, 4), (use_far, 1, 2), (use_own, 1, 2), (use_first, 0, 0),
+        (use_first, 1, 0), (give_cols, 1), (use_own, 0, 2), (use_far, 0, 2), (use_first, 0, 2), (pass_cols, 1),
+        (give_cols, 0), (pass_cols, 0), (weight_step, 5), (weight_step, 6),
     ):
         step[0](*step[1:])
-
-    def cols1(h):
-        return copy(col_out.at[h], col_in.at[h], c_s, c_r.at[h], cores)
-
-    cols2 = copy(col2_out, col2_in, c2_s, c2_r, across)
-
-    def give_cols(h):
-        for p in range(2):
-            col_out[h, p] = terms[p, 2 * h + 1 - core].astype(BF16)
-        cols1(h).start()
-
-    give_cols(1 - high)
-    give_cols(high)
-    cols1(1 - high).wait_recv()
-    for p in range(2):
-        col2_out[p] = (terms[p, row_across] + col_in[1 - high, p].astype(F32)).astype(BF16)
-    cols2.start()
-    weight_step(5)
-    weight_step(6)
 
     def sent(ref, sem):
         copy(ref, ref, sem, sem, pair).wait_send()
@@ -526,15 +560,13 @@
     sent(grads.at[0, 0], g_s.at[5])
     for step in weight_all:
         step.wait_send()
-    gives[0].wait()
-    gives[1].wait()
-
-    cols1(high).wait_recv()
-    cols2.wait_recv()
+
     contract = (((1,), (1,)), ((), ()))
     total = jnp.zeros((NODES, WIDTH), F32)
-    for p in range(2):
-        value = (terms[p, row] + col_in[high, p].astype(F32) + col2_in[p].astype(F32)).T
+    for p in (1, 0):
+        cols1(p, high).wait_recv()
+        cols2(p).wait_recv()
+        value = (terms[p, row] + col_in[p, high].astype(F32) + col2_in[p].astype(F32)).T
         for part in split(value):
             total = total + lax.dot_general(
                 part, weight[:, p * HALF:(p + 1) * HALF], contract, preferred_element_type=F32
@@ -542,8 +574,9 @@
     grad_features[...] = total.astype(BF16)
     gives[2].start()
     sent(col_out, c_s)
-    cols2.wait_send()
-    gives[2].wait()
+    sent(col2_out, c2_s)
+    for give in gives:
+        give.wait()
 
 
 def layer(features, features_across, weight, dense, output_grad):
@@ -580,13 +613,13 @@
             f32(2, PEERS, HALF, NODES),
             bf(2, 2, HALF, NODES), bf(2, 2, HALF, NODES),
             bf(2, HALF, NODES), bf(2, HALF, NODES),
-            bf(HALF, WIDTH), bf(HALF, WIDTH),
+            f32(HALF, WIDTH), f32(HALF, WIDTH),
             f32(4, 64, WIDTH),
-            bf(3, 64, WIDTH), bf(3, 64, WIDTH),
+            f32(3, 64, WIDTH),
             f32(16, 16, TILE), f32(16, 16, TILE),
             bf(16, 16, TILE),
             bf(2, 4, 64, WIDTH),
-            dma((LOADS,)), dma((4,)), dma((3,)),
+            dma((4, 4, 2)), dma((4,)), dma((3,)),
             dma((2,)), dma((2,)),
             dma, dma((2, 4)),
             dma, dma((2, 4, 2)),
@@ -595,12 +628,12 @@
             dma, dma((2, 2)),
             dma, dma((2,)),
             dma((6,)), dma((2,)), dma((2, 3, 2)), dma((2, 2, 4, 2)), dma((2, 4)), dma((2, 4)),
+            dma, dma((2, 2)),
             dma, dma((2,)),
-            dma, dma,
             dma((6,)), dma((6,)),
         ],
         compiler_params=pltpu.CompilerParams(
-            collective_id=0, has_side_effects=True, vmem_limit_bytes=62 * 2**20
+            collective_id=0, has_side_effects=True, vmem_limit_bytes=LAYER_VMEM
         ),
         name="layer",
     )(features, features_across, weight, dense, output_grad)
@@ -623,7 +656,7 @@
         ),
         in_specs=[vmem] * 3,
         out_specs=(vmem,) * 3,
-        compiler_params=pltpu.CompilerParams(vmem_limit_bytes=63 * 2**20),
+        compiler_params=pltpu.CompilerParams(vmem_limit_bytes=FINISH_VMEM),
         name="finish",
     )(output, grad_features, grad_weight)
 

time: 128 us -> 126 us (0.984)
  Pallas kernels: 122 us -> 120 us
  transfers between devices with their start and end apart: 1 -> 1, of which waited for: 0 -> 0; matrix products, arithmetic and copies ran while one was open for 0% -> 0% of each run, Pallas kernels for 9% -> 8%
where the time goes in v3:
time: 126 us
  Pallas kernels  120 us (95%)
  starting transfers between devices  3.82 us (3%)
  between operations  1.32 us (1%)
    pallas_call x1, Pallas kernels, layer(): pl.pallas_call(layer_kernel, out_shape=(jax.ShapeDtypeStruct((NODES, WIDT...  107 us
    pallas_call x1, Pallas kernels, place_tiles(): pl.pallas_call(place_kernel, out_shape=jax.ShapeDtypeStruct((CHUNKS * NOD...  10.7 us
    ppermute x1, starting transfers between devices, per_device(): lax.ppermute(features, 'row', [(r, (r + 2) % PEERS) for r in range(PEERS)])  3.82 us
  transfers between devices with their start and end apart: 1, of which 0 were waited for; matrix products, arithmetic and copies ran while one was open for 0% of the time, Pallas kernels for 8%

profile of v3, /device:TPU:1, one launch (start us, length us, event | category | flops | bytes accessed | tf_op | source)
XLA Modules:
  0.0 125.6 jit_solution(13856765298751427193)
XLA Ops:
  0.6 3.8 %collective-permute-start = (bf16[256,512]{1,0:T(8,128)(2,1)}, bf16[256,512]{1,0:T(8,128)(2,1)S(1)}, u32[]{:S(2)}, u32[]{:S(2)}) collective-permute-start(bf16[256,512]{1,0:T(8,128)(2,1)} %features.1), channel_id=1, source_target_pairs={{0,64},{32,96},{64,0},{96,32},{1,65},{33,97},{65,1},{97,33},{2,66}... | collective-permute-start | bytes 786440 | tf_op jit(solution)/shard_map/ppermute | solution.py:665
  5.1 10.7 %place_tiles.1.dense_hbm = bf16[8192,1024]{1,0:T(8,128)(2,1)} custom-call(s32[192]{0:T(256)} %rows.1, s32[192]{0:T(256)} %cols.1, s32[1]{0:T(128)S(6)} %copy.10.count, bf16[192,128,128]{2,1,0:T(8,128)(2,1)} %values.1), custom_call_target="tpu_custom_call" | custom-call | bytes 31457280 | tf_op jit(solution)/shard_map/place_tiles/pallas_call | solution.py:70
  15.8 0.0 collective-permute-done.features_across
  15.8 0.0 copy-start
  15.8 0.7 copy-done
  16.5 106.6 %layer.1 = (bf16[256,512]{1,0:T(8,128)(2,1)}, bf16[256,512]{1,0:T(8,128)(2,1)}, bf16[2,4,64,512]{3,2,1,0:T(8,128)(2,1)}) custom-call(bf16[256,512]{1,0:T(8,128)(2,1)} %features.1, bf16[256,512]{1,0:T(8,128)(2,1)} %copy-done, bf16[512,512]{1,0:T(8,128)(2,1)} %weight_hbm.1, bf16[8192,1024]{1,0:T(8,128)(2,1)} %place_tiles.1.dense_hbm, ...), custom_call_target="tpu_custom_call" | custom-call | tf_op jit(solution)/shard_map/layer/pallas_call | solution.py:588
  123.1 2.5 %finish.1 = (bf16[256,512]{1,0:T(8,128)(2,1)}, bf16[256,512]{1,0:T(8,128)(2,1)}, f32[512,512]{1,0:T(8,128)}) custom-call(bf16[256,512]{1,0:T(8,128)(2,1)} %get-tuple-element.6.first_in, bf16[256,512]{1,0:T(8,128)(2,1)} %get-tuple-element.7.second_in, bf16[512,512]{1,0:T(8,128)(2,1)} %bitcast.1), custom_call_target="tpu_custom_call" | custom-call | tf_op jit(solution)/shard_map/finish/pallas_call | solution.py:650
Async XLA Ops:
  0.6 15.2 %collective-permute-start = (bf16[256,512]{1,0:T(8,128)(2,1)}, bf16[256,512]{1,0:T(8,128)(2,1)S(1)}, u32[]{:S(2)}, u32[]{:S(2)}) collective-permute-start(bf16[256,512]{1,0:T(8,128)(2,1)} %features.1), channel_id=1, source_target_pairs={{0,64},{32,96},{64,0},{96,32},{1,65},{33,97},{65,1},{97,33},{2,66}... | collective-permute-start | bytes 786440 | tf_op jit(solution)/shard_map/ppermute | solution.py:665
  15.8 0.7 copy-start

commit v4 on v3

--- a/solution.py
+++ b/solution.py
@@ -50,15 +50,30 @@
         band = pl.ds(pl.multiple_of(g * BAND_TILES * TILE, BAND_TILES * TILE), BAND_TILES * TILE)
         return pltpu.make_async_copy(block.at[band], dense.at[band], out_sem.at[g])
 
+    def spot_of(t):
+        row = pl.multiple_of(rows[t] * TILE, TILE)
+        col = pl.multiple_of(cols[t] * TILE, TILE)
+        return row, col, (pl.ds(row, TILE), pl.ds(col, TILE))
+
     for g in range(BANDS):
-        def place(i, carry):
-            t = listed[g, i]
-            row = pl.ds(pl.multiple_of(rows[t] * TILE, TILE), TILE)
-            col = pl.ds(pl.multiple_of(cols[t] * TILE, TILE), TILE)
-            block[row, col] = block[row, col] + tiles[t]
+        def place_two(i, carry):
+            t, u = listed[g, 2 * i], listed[g, 2 * i + 1]
+            row_t, col_t, at_t = spot_of(t)
+            row_u, col_u, at_u = spot_of(u)
+            first, second = block[at_t] + tiles[t], block[at_u]
+            second = jnp.where((row_t == row_u) & (col_t == col_u), first, second) + tiles[u]
+            block[at_t] = first
+            block[at_u] = second
             return carry
 
-        lax.fori_loop(0, filled[g], place, 0)
+        def place_last(i, carry):
+            t = listed[g, filled[g] - 1]
+            at_t = spot_of(t)[2]
+            block[at_t] = block[at_t] + tiles[t]
+            return carry
+
+        lax.fori_loop(0, filled[g] // 2, place_two, 0)
+        lax.fori_loop(0, filled[g] % 2, place_last, 0)
         store(g).start()
     for g in range(BANDS):
         store(g).wait()

time: 126 us -> 126 us (level)
    pallas_call x1, Pallas kernels: 107 us -> 108 us  [layer(): pl.pallas_call(layer_kernel, out_shape=(jax.ShapeDtypeStruct((NODES, WIDT...]
where the time goes in v4:
time: 126 us
  Pallas kernels  120 us (95%)
  starting transfers between devices  3.82 us (3%)
  between operations  1.32 us (1%)
    pallas_call x1, Pallas kernels, layer(): pl.pallas_call(layer_kernel, out_shape=(jax.ShapeDtypeStruct((NODES, WIDT...  108 us
    pallas_call x1, Pallas kernels, place_tiles(): pl.pallas_call(place_kernel, out_shape=jax.ShapeDtypeStruct((CHUNKS * NOD...  9.5 us
    ppermute x1, starting transfers between devices, per_device(): lax.ppermute(features, 'row', [(r, (r + 2) % PEERS) for r in range(PEERS)])  3.82 us
  transfers between devices with their start and end apart: 1, of which 0 were waited for; matrix products, arithmetic and copies ran while one was open for 0% of the time, Pallas kernels for 8%

profile of v4, /device:TPU:1, one launch (start us, length us, event | category | flops | bytes accessed | tf_op | source)
XLA Modules:
  0.0 125.9 jit_solution(13488655328345729672)
XLA Ops:
  0.6 3.8 %collective-permute-start = (bf16[256,512]{1,0:T(8,128)(2,1)}, bf16[256,512]{1,0:T(8,128)(2,1)S(1)}, u32[]{:S(2)}, u32[]{:S(2)}) collective-permute-start(bf16[256,512]{1,0:T(8,128)(2,1)} %features.1), channel_id=1, source_target_pairs={{0,64},{32,96},{64,0},{96,32},{1,65},{33,97},{65,1},{97,33},{2,66}... | collective-permute-start | bytes 786440 | tf_op jit(solution)/shard_map/ppermute | solution.py:680
  5.1 9.5 %place_tiles.1.dense_hbm = bf16[8192,1024]{1,0:T(8,128)(2,1)} custom-call(s32[192]{0:T(256)} %rows.1, s32[192]{0:T(256)} %cols.1, s32[1]{0:T(128)S(6)} %copy.10.count, bf16[192,128,128]{2,1,0:T(8,128)(2,1)} %values.1), custom_call_target="tpu_custom_call" | custom-call | bytes 31457280 | tf_op jit(solution)/shard_map/place_tiles/pallas_call | solution.py:85
  14.6 0.0 collective-permute-done.features_across
  14.6 0.0 copy-start
  14.6 0.7 copy-done
  15.3 108.1 %layer.1 = (bf16[256,512]{1,0:T(8,128)(2,1)}, bf16[256,512]{1,0:T(8,128)(2,1)}, bf16[2,4,64,512]{3,2,1,0:T(8,128)(2,1)}) custom-call(bf16[256,512]{1,0:T(8,128)(2,1)} %features.1, bf16[256,512]{1,0:T(8,128)(2,1)} %copy-done, bf16[512,512]{1,0:T(8,128)(2,1)} %weight_hbm.1, bf16[8192,1024]{1,0:T(8,128)(2,1)} %place_tiles.1.dense_hbm, ...), custom_call_target="tpu_custom_call" | custom-call | tf_op jit(solution)/shard_map/layer/pallas_call | solution.py:603
  123.4 2.5 %finish.1 = (bf16[256,512]{1,0:T(8,128)(2,1)}, bf16[256,512]{1,0:T(8,128)(2,1)}, f32[512,512]{1,0:T(8,128)}) custom-call(bf16[256,512]{1,0:T(8,128)(2,1)} %get-tuple-element.6.first_in, bf16[256,512]{1,0:T(8,128)(2,1)} %get-tuple-element.7.second_in, bf16[512,512]{1,0:T(8,128)(2,1)} %bitcast.1), custom_call_target="tpu_custom_call" | custom-call | tf_op jit(solution)/shard_map/finish/pallas_call | solution.py:665
Async XLA Ops:
  0.6 14.0 %collective-permute-start = (bf16[256,512]{1,0:T(8,128)(2,1)}, bf16[256,512]{1,0:T(8,128)(2,1)S(1)}, u32[]{:S(2)}, u32[]{:S(2)}) collective-permute-start(bf16[256,512]{1,0:T(8,128)(2,1)} %features.1), channel_id=1, source_target_pairs={{0,64},{32,96},{64,0},{96,32},{1,65},{33,97},{65,1},{97,33},{2,66}... | collective-permute-start | bytes 786440 | tf_op jit(solution)/shard_map/ppermute | solution.py:680
  14.6 0.7 copy-start

commit v5 on v3

--- a/solution.py
+++ b/solution.py
@@ -98,10 +98,10 @@
 def layer_kernel(
     features, features_across, weight_hbm, dense_hbm, output_grad_hbm, output_hbm, grad_features_hbm, grad_weight_hbm,
     dense, feats, weight, output_grad, output, grad_features, lifted,
-    pairs_out, pairs_in, far_out, far_in, near_out, near_in, far2_out, far2_in, near2_out, near2_in, pair_out, pair_in,
+    pairs_out, pairs_in, far_out, far_in, near_out, near_in, pairs2_out, pairs2_in, far2_out, far2_in, near2_out, near2_in, pair_out, pair_in,
     kept, grads, terms, col_out, col_in, col2_out, col2_in,
     wcore_out, wcore_in, wsum, wy_in, wgrid, wgrid_in, ggrid, wfull,
-    load_sem, in_sem, out_sem, a_s, a_r, pairs_s, pairs_r, far_s, far_r, near_s, near_r, far2_s, far2_r, near2_s, near2_r,
+    load_sem, in_sem, out_sem, a_s, a_r, pairs_s, pairs_r, far_s, far_r, near_s, near_r, pairs2_s, pairs2_r, far2_s, far2_r, near2_s, near2_r,
     pair_s, pair_r, g_s, own_r, second_r, first_r, gfar_r, gpair_r, c_s, c_r, c2_s, c2_r, w_s, w_r,
 ):
     row, z, rep = lax.axis_index("row"), lax.axis_index("col"), lax.axis_index("rep")
@@ -155,10 +155,8 @@
         sem = load_sem.at[i, j, 0 if pair_ is mine else 1]
         return pltpu.make_async_copy(dense_hbm.at[span], dense.at[span], sem)
 
-    uses = [(steps[d], o, other) for o in (0,) for d in range(2)]
-    uses += [(2, 2, other)] + [(steps[d], 2, other) for d in range(2)] + [(steps[d], 1, other) for d in range(2)]
-    uses += [(2, 1, other), (2, 2, mine)] + [(steps[d], 3, other) for d in range(2)] + [(2, 3, other)]
-    uses += [(steps[d], 2, mine) for d in range(2)]
+    uses = [(2, 1, other)] + [(steps[d], 0, other) for d in range(2)] + [(2, 2, other)]
+    uses += [(steps[d], o, other) for o in (2, 1) for d in range(2)] + [(2, 3, other), (2, 0, other), (2, 1, mine)]
     waiting = []
     for i, j, pair_ in uses + [(i, j, pair_) for pair_ in (other, mine) for i in range(4) for j in range(4)]:
         for key in ((i, j, pair_), (j, i, pair_)):
@@ -261,35 +259,48 @@
             near_out[p, o, 0, d, rest] = value[rest].astype(BF16)
             near(p, o, 0, d).start()
 
+    def pairs2(p):
+        return copy(pairs2_out.at[p], pairs2_in.at[p], pairs2_s, pairs2_r.at[p], pair)
+
     def far2(p, d):
-        return copy(far2_out.at[p, d], far2_in.at[p, d], far2_s, far2_r.at[p, d], along(axes[p][1], 3 - 2 * d))
-
-    def near2(p, d, y):
-        return copy(near2_out.at[p, y, d], near2_in.at[p, y, d], near2_s, near2_r.at[p, y], along(axes[p][1], 3 - 2 * d))
-
-    def near2_both(p, y):
-        return copy(near2_out.at[p, y], near2_in.at[p, y], near2_s, near2_r.at[p, y], pair)
+        half = pl.ds(d * TILE, TILE)
+        return copy(far2_out.at[p, half], far2_in.at[p, d], far2_s, far2_r.at[p, d], along(axes[p][1], steps[d]))
+
+    def near2(p, r, d):
+        return copy(near2_out.at[p, r, d], near2_in.at[p, r, d], near2_s, near2_r.at[p, r], along(axes[p][1], steps[d]))
+
+    def near2_both(p, r):
+        return copy(near2_out.at[p, r], near2_in.at[p, r], near2_s, near2_r.at[p, r], pair)
 
     def first_sum(p, o, y):
         need_all()
         value = partial(p, spots[p][0], (spots[p][1] + o) % 4, y)
-        r = (y + low) % 2
+        r = 0 if y is mine else 1
         near_both(p, o, r).wait_recv()
         return value + near_in[p, o, r, 0].astype(F32) + near_in[p, o, r, 1].astype(F32)
 
-    def send_far2(p, d):
-        far2_out[p, d] = first_sum(p, 2, d).astype(BF16)
-        far2(p, d).start()
+    def send_pair2(p):
+        pairs2_out[p] = first_sum(p, 2, other).astype(BF16)
+        pairs2(p).start()
+
+    def send_far2(p):
+        value = first_sum(p, 2, mine)
+        pairs2(p).wait_recv()
+        far2_out[p] = (value + pairs2_in[p].astype(F32)).astype(BF16)
+        for d in range(2):
+            far2(p, d).start()
 
     def send_other2(p, d):
-        near2_out[p, 1 - d, d] = first_sum(p, 3 - 2 * d, 1 - d).astype(BF16)
-        near2(p, d, 1 - d).start()
+        near2_out[p, 1, d] = first_sum(p, steps[d], other).astype(BF16)
+        near2(p, 1, d).start()
 
     def send_mine2(p, d):
-        value = first_sum(p, 3 - 2 * d, d)
+        value = first_sum(p, steps[d], mine)
         far2(p, d).wait_recv()
-        near2_out[p, d, d] = (value + far2_in[p, d].astype(F32)).astype(BF16)
-        near2(p, d, d).start()
+        half, rest = (slice(0, TILE), slice(TILE, NODES))[::1 - 2 * d]
+        near2_out[p, 0, d, half] = (value[half] + far2_in[p, d].astype(F32)).astype(BF16)
+        near2_out[p, 0, d, rest] = value[rest].astype(BF16)
+        near2(p, 0, d).start()
 
     def keep(p, y):
         kept[p, y] = first_sum(p, 0, y)
@@ -298,8 +309,9 @@
         return copy(pair_out.at[p], pair_in.at[p], pair_s, pair_r.at[p], pair)
 
     def second_sum(p, y):
-        near2_both(p, y).wait_recv()
-        return kept[p, y] + near2_in[p, y, 0].astype(F32) + near2_in[p, y, 1].astype(F32)
+        r = 0 if y is mine else 1
+        near2_both(p, r).wait_recv()
+        return kept[p, y] + near2_in[p, r, 0].astype(F32) + near2_in[p, r, 1].astype(F32)
 
     def send_last(p):
         pair_out[p] = second_sum(p, other).astype(BF16)
@@ -309,10 +321,10 @@
         kept[p, mine] = second_sum(p, mine)
 
     for step in (
-        (send_other, 0), (send_pair, 2), (send_other, 2), (send_other, 1), (send_pair, 1), (send_far, 2), (send_other, 3),
-        (send_pair, 3), (send_mine, 2), (keep, other), (send_far2, other), (send_pair, 0), (send_far, 1), (send_other2, mine),
-        (send_far, 3), (send_far2, mine), (send_mine2, other), (send_mine, 1), (send_far, 0), (send_mine, 3), (send_mine, 0),
-        (send_last,), (send_other2, other), (send_mine2, mine), (keep, mine), (keep_last,),
+        (send_pair, 1), (send_other, 0), (send_pair, 2), (send_other, 2), (send_other, 1), (send_pair, 3), (send_pair, 0),
+        (send_far, 1), (send_pair2,), (send_other, 3), (send_far, 2), (send_mine, 1), (send_mine, 2), (send_far, 3),
+        (send_other2, 1), (send_other2, 0), (send_far, 0), (send_mine, 3), (keep, other), (send_far2,), (send_mine, 0),
+        (send_last,), (send_mine2, 0), (send_mine2, 1), (keep, mine), (keep_last,),
     ):
         for p in range(2):
             step[0](p, *step[1:])
@@ -549,6 +561,7 @@
     sent(pairs_out, pairs_s)
     sent(far_out, far_s)
     sent(near_out, near_s)
+    sent(pairs2_out, pairs2_s)
     sent(far2_out, far2_s)
     sent(near2_out, near2_s)
     sent(pair_out, pair_s)
@@ -605,7 +618,8 @@
             bf(2, 4, *block), bf(2, 4, *block),
             bf(2, 4, *block), bf(2, 4, 2, TILE, HALF),
             bf(2, 4, 2, 2, *block), bf(2, 4, 2, 2, *block),
-            bf(2, 2, *block), bf(2, 2, *block),
+            bf(2, *block), bf(2, *block),
+            bf(2, *block), bf(2, 2, TILE, HALF),
             bf(2, 2, 2, *block), bf(2, 2, 2, *block),
             bf(2, *block), bf(2, *block),
             f32(2, 2, *block),
@@ -624,6 +638,7 @@
             dma, dma((2, 4)),
             dma, dma((2, 4, 2)),
             dma, dma((2, 4, 2)),
+            dma, dma((2,)),
             dma, dma((2, 2)),
             dma, dma((2, 2)),
             dma, dma((2,)),

time: 126 us -> 125 us (level)
    pallas_call x1, Pallas kernels: 107 us -> 105 us  [layer(): pl.pallas_call(layer_kernel, out_shape=(jax.ShapeDtypeStruct((NODES, WIDT...]
  transfers between devices with their start and end apart: 1 -> 1, of which waited for: 0 -> 0; matrix products, arithmetic and copies ran while one was open for 0% -> 0% of each run, Pallas kernels for 8% -> 9%
where the time goes in v5:
time: 125 us; the launch traced here: 124 us
  Pallas kernels  119 us (95%)
  starting transfers between devices  3.82 us (3%)
  between operations  1.32 us (1%)
    pallas_call x1, Pallas kernels, layer(): pl.pallas_call(layer_kernel, out_shape=(jax.ShapeDtypeStruct((NODES, WIDT...  105 us
    pallas_call x1, Pallas kernels, place_tiles(): pl.pallas_call(place_kernel, out_shape=jax.ShapeDtypeStruct((CHUNKS * NOD...  10.9 us
    ppermute x1, starting transfers between devices, per_device(): lax.ppermute(features, 'row', [(r, (r + 2) % PEERS) for r in range(PEERS)])  3.82 us
    pallas_call x1, Pallas kernels, finish(): pl.pallas_call(finish_kernel, out_shape=(jax.ShapeDtypeStruct(output.shap...  2.52 us
  transfers between devices with their start and end apart: 1, of which 0 were waited for; matrix products, arithmetic and copies ran while one was open for 0% of the time, Pallas kernels for 9%

profile of v5, /device:TPU:1, one launch (start us, length us, event | category | flops | bytes accessed | tf_op | source)
XLA Modules:
  0.0 124.5 jit_solution(6839094086860925481)
XLA Ops:
  0.6 3.8 %collective-permute-start = (bf16[256,512]{1,0:T(8,128)(2,1)}, bf16[256,512]{1,0:T(8,128)(2,1)S(1)}, u32[]{:S(2)}, u32[]{:S(2)}) collective-permute-start(bf16[256,512]{1,0:T(8,128)(2,1)} %features.1), channel_id=1, source_target_pairs={{0,64},{32,96},{64,0},{96,32},{1,65},{33,97},{65,1},{97,33},{2,66}... | collective-permute-start | bytes 786440 | tf_op jit(solution)/shard_map/ppermute | solution.py:680
  5.1 10.9 %place_tiles.1.dense_hbm = bf16[8192,1024]{1,0:T(8,128)(2,1)} custom-call(s32[192]{0:T(256)} %rows.1, s32[192]{0:T(256)} %cols.1, s32[1]{0:T(128)S(6)} %copy.10.count, bf16[192,128,128]{2,1,0:T(8,128)(2,1)} %values.1), custom_call_target="tpu_custom_call" | custom-call | bytes 31457280 | tf_op jit(solution)/shard_map/place_tiles/pallas_call | solution.py:70
  16.0 0.0 collective-permute-done.features_across
  16.0 0.0 copy-start
  16.0 0.7 copy-done
  16.7 105.2 %layer.1 = (bf16[256,512]{1,0:T(8,128)(2,1)}, bf16[256,512]{1,0:T(8,128)(2,1)}, bf16[2,4,64,512]{3,2,1,0:T(8,128)(2,1)}) custom-call(bf16[256,512]{1,0:T(8,128)(2,1)} %features.1, bf16[256,512]{1,0:T(8,128)(2,1)} %copy-done, bf16[512,512]{1,0:T(8,128)(2,1)} %weight_hbm.1, bf16[8192,1024]{1,0:T(8,128)(2,1)} %place_tiles.1.dense_hbm, ...), custom_call_target="tpu_custom_call" | custom-call | tf_op jit(solution)/shard_map/layer/pallas_call | solution.py:601
  122.0 2.5 %finish.1 = (bf16[256,512]{1,0:T(8,128)(2,1)}, bf16[256,512]{1,0:T(8,128)(2,1)}, f32[512,512]{1,0:T(8,128)}) custom-call(bf16[256,512]{1,0:T(8,128)(2,1)} %get-tuple-element.6.first_in, bf16[256,512]{1,0:T(8,128)(2,1)} %get-tuple-element.7.second_in, bf16[512,512]{1,0:T(8,128)(2,1)} %bitcast.1), custom_call_target="tpu_custom_call" | custom-call | tf_op jit(solution)/shard_map/finish/pallas_call | solution.py:665
Async XLA Ops:
  0.6 15.4 %collective-permute-start = (bf16[256,512]{1,0:T(8,128)(2,1)}, bf16[256,512]{1,0:T(8,128)(2,1)S(1)}, u32[]{:S(2)}, u32[]{:S(2)}) collective-permute-start(bf16[256,512]{1,0:T(8,128)(2,1)} %features.1), channel_id=1, source_target_pairs={{0,64},{32,96},{64,0},{96,32},{1,65},{33,97},{65,1},{97,33},{2,66}... | collective-permute-start | bytes 786440 | tf_op jit(solution)/shard_map/ppermute | solution.py:680
  16.0 0.7 copy-start

commit v6 on v5

--- a/solution.py
+++ b/solution.py
@@ -654,14 +654,29 @@
     )(features, features_across, weight, dense, output_grad)
 
 
-def finish_kernel(first_in, second_in, weight_in, first, second, weight):
-    first[...] = first_in[...]
-    second[...] = second_in[...]
-    weight[...] = weight_in[...].astype(F32).T
+def finish_kernel(first_in, second_in, weight_in, first, second, weight, first_at, second_at, weight_at, turned, in_sem, out_sem):
+    loads = [
+        pltpu.make_async_copy(src, dst, in_sem.at[i])
+        for i, (src, dst) in enumerate(((weight_in, weight_at), (first_in, first_at), (second_in, second_at)))
+    ]
+    stores = [
+        pltpu.make_async_copy(src, dst, out_sem.at[i])
+        for i, (src, dst) in enumerate(((turned, weight), (first_at, first), (second_at, second)))
+    ]
+    for load in loads:
+        load.start()
+    loads[0].wait()
+    turned[...] = weight_at[...].astype(F32).T
+    stores[0].start()
+    for load, store in zip(loads[1:], stores[1:]):
+        load.wait()
+        store.start()
+    for store in stores:
+        store.wait()
 
 
 def finish(output, grad_features, grad_weight):
-    vmem = pl.BlockSpec(memory_space=pltpu.VMEM)
+    anywhere = pl.BlockSpec(memory_space=pl.ANY)
     return pl.pallas_call(
         finish_kernel,
         out_shape=(
@@ -669,8 +684,16 @@
             jax.ShapeDtypeStruct(grad_features.shape, BF16),
             jax.ShapeDtypeStruct(grad_weight.shape, F32),
         ),
-        in_specs=[vmem] * 3,
-        out_specs=(vmem,) * 3,
+        in_specs=[anywhere] * 3,
+        out_specs=(anywhere,) * 3,
+        scratch_shapes=[
+            pltpu.VMEM(output.shape, BF16),
+            pltpu.VMEM(grad_features.shape, BF16),
+            pltpu.VMEM(grad_weight.shape, BF16),
+            pltpu.VMEM(grad_weight.shape, F32),
+            pltpu.SemaphoreType.DMA((3,)),
+            pltpu.SemaphoreType.DMA((3,)),
+        ],
         compiler_params=pltpu.CompilerParams(vmem_limit_bytes=FINISH_VMEM),
         name="finish",
     )(output, grad_features, grad_weight)

time: 125 us -> 125 us (level)
  transfers between devices with their start and end apart: 1 -> 1, of which waited for: 0 -> 0; matrix products, arithmetic and copies ran while one was open for 0% -> 0% of each run, Pallas kernels for 9% -> 8%
where the time goes in v6:
time: 125 us
  Pallas kernels  119 us (95%)
  starting transfers between devices  3.82 us (3%)
  between operations  1.48 us (1%)
    pallas_call x1, Pallas kernels, layer(): pl.pallas_call(layer_kernel, out_shape=(jax.ShapeDtypeStruct((NODES, WIDT...  106 us
    pallas_call x1, Pallas kernels, place_tiles(): pl.pallas_call(place_kernel, out_shape=jax.ShapeDtypeStruct((CHUNKS * NOD...  10.6 us
    ppermute x1, starting transfers between devices, per_device(): lax.ppermute(features, 'row', [(r, (r + 2) % PEERS) for r in range(PEERS)])  3.82 us
  transfers between devices with their start and end apart: 1, of which 0 were waited for; matrix products, arithmetic and copies ran while one was open for 0% of the time, Pallas kernels for 8%

profile of v6, /device:TPU:1, one launch (start us, length us, event | category | flops | bytes accessed | tf_op | source)
XLA Modules:
  0.0 125.2 jit_solution(3103330715447464888)
XLA Ops:
  0.6 3.8 %collective-permute-start = (bf16[256,512]{1,0:T(8,128)(2,1)}, bf16[256,512]{1,0:T(8,128)(2,1)S(1)}, u32[]{:S(2)}, u32[]{:S(2)}) collective-permute-start(bf16[256,512]{1,0:T(8,128)(2,1)} %features.1), channel_id=1, source_target_pairs={{0,64},{32,96},{64,0},{96,32},{1,65},{33,97},{65,1},{97,33},{2,66}... | collective-permute-start | bytes 786440 | tf_op jit(solution)/shard_map/ppermute | solution.py:703
  5.1 10.6 %place_tiles.1.dense_hbm = bf16[8192,1024]{1,0:T(8,128)(2,1)} custom-call(s32[192]{0:T(256)} %rows.1, s32[192]{0:T(256)} %cols.1, s32[1]{0:T(128)S(6)} %copy.10.count, bf16[192,128,128]{2,1,0:T(8,128)(2,1)} %values.1), custom_call_target="tpu_custom_call" | custom-call | bytes 31457280 | tf_op jit(solution)/shard_map/place_tiles/pallas_call | solution.py:70
  15.7 0.0 collective-permute-done.features_across
  15.7 0.0 copy-start
  15.7 0.7 copy-done
  16.4 106.2 %layer.1 = (bf16[256,512]{1,0:T(8,128)(2,1)}, bf16[256,512]{1,0:T(8,128)(2,1)}, bf16[2,4,64,512]{3,2,1,0:T(8,128)(2,1)}) custom-call(bf16[256,512]{1,0:T(8,128)(2,1)} %features.1, bf16[256,512]{1,0:T(8,128)(2,1)} %copy-done, bf16[512,512]{1,0:T(8,128)(2,1)} %weight_hbm.1, bf16[8192,1024]{1,0:T(8,128)(2,1)} %place_tiles.1.dense_hbm, ...), custom_call_target="tpu_custom_call" | custom-call | tf_op jit(solution)/shard_map/layer/pallas_call | solution.py:601
  122.6 2.5 %finish.1 = (bf16[256,512]{1,0:T(8,128)(2,1)}, bf16[256,512]{1,0:T(8,128)(2,1)}, f32[512,512]{1,0:T(8,128)}) custom-call(bf16[256,512]{1,0:T(8,128)(2,1)} %get-tuple-element.6.first_in, bf16[256,512]{1,0:T(8,128)(2,1)} %get-tuple-element.7.second_in, bf16[512,512]{1,0:T(8,128)(2,1)} %bitcast.1), custom_call_target="tpu_custom_call" | custom-call | tf_op jit(solution)/shard_map/finish/pallas_call | solution.py:680
Async XLA Ops:
  0.6 15.1 %collective-permute-start = (bf16[256,512]{1,0:T(8,128)(2,1)}, bf16[256,512]{1,0:T(8,128)(2,1)S(1)}, u32[]{:S(2)}, u32[]{:S(2)}) collective-permute-start(bf16[256,512]{1,0:T(8,128)(2,1)} %features.1), channel_id=1, source_target_pairs={{0,64},{32,96},{64,0},{96,32},{1,65},{33,97},{65,1},{97,33},{2,66}... | collective-permute-start | bytes 786440 | tf_op jit(solution)/shard_map/ppermute | solution.py:703
  15.7 0.7 copy-start

commit v7 on v6

--- a/solution.py
+++ b/solution.py
@@ -50,15 +50,30 @@
         band = pl.ds(pl.multiple_of(g * BAND_TILES * TILE, BAND_TILES * TILE), BAND_TILES * TILE)
         return pltpu.make_async_copy(block.at[band], dense.at[band], out_sem.at[g])
 
+    def spot_of(t):
+        row = pl.multiple_of(rows[t] * TILE, TILE)
+        col = pl.multiple_of(cols[t] * TILE, TILE)
+        return row, col, (pl.ds(row, TILE), pl.ds(col, TILE))
+
     for g in range(BANDS):
-        def place(i, carry):
-            t = listed[g, i]
-            row = pl.ds(pl.multiple_of(rows[t] * TILE, TILE), TILE)
-            col = pl.ds(pl.multiple_of(cols[t] * TILE, TILE), TILE)
-            block[row, col] = block[row, col] + tiles[t]
+        def place_two(i, carry):
+            t, u = listed[g, 2 * i], listed[g, 2 * i + 1]
+            row_t, col_t, at_t = spot_of(t)
+            row_u, col_u, at_u = spot_of(u)
+            first, second = block[at_t] + tiles[t], block[at_u]
+            second = jnp.where((row_t == row_u) & (col_t == col_u), first, second) + tiles[u]
+            block[at_t] = first
+            block[at_u] = second
             return carry
 
-        lax.fori_loop(0, filled[g], place, 0)
+        def place_last(i, carry):
+            t = listed[g, filled[g] - 1]
+            at_t = spot_of(t)[2]
+            block[at_t] = block[at_t] + tiles[t]
+            return carry
+
+        lax.fori_loop(0, filled[g] // 2, place_two, 0)
+        lax.fori_loop(0, filled[g] % 2, place_last, 0)
         store(g).start()
     for g in range(BANDS):
         store(g).wait()

time: 125 us -> 125 us (level)
    pallas_call x1, Pallas kernels: 106 us -> 105 us  [layer(): pl.pallas_call(layer_kernel, out_shape=(jax.ShapeDtypeStruct((NODES, WIDT...]
  transfers between devices with their start and end apart: 1 -> 1, of which waited for: 0 -> 0; matrix products, arithmetic and copies ran while one was open for 0% -> 0% of each run, Pallas kernels for 8% -> 9%
where the time goes in v7:
time: 125 us
  Pallas kernels  119 us (95%)
  starting transfers between devices  3.82 us (3%)
  between operations  1.48 us (1%)
    pallas_call x1, Pallas kernels, layer(): pl.pallas_call(layer_kernel, out_shape=(jax.ShapeDtypeStruct((NODES, WIDT...  105 us
    pallas_call x1, Pallas kernels, place_tiles(): pl.pallas_call(place_kernel, out_shape=jax.ShapeDtypeStruct((CHUNKS * NOD...  11.2 us
    ppermute x1, starting transfers between devices, per_device(): lax.ppermute(features, 'row', [(r, (r + 2) % PEERS) for r in range(PEERS)])  3.82 us
  transfers between devices with their start and end apart: 1, of which 0 were waited for; matrix products, arithmetic and copies ran while one was open for 0% of the time, Pallas kernels for 9%

profile of v7, /device:TPU:1, one launch (start us, length us, event | category | flops | bytes accessed | tf_op | source)
XLA Modules:
  0.0 124.5 jit_solution(14518218898585720635)
XLA Ops:
  0.6 3.8 %collective-permute-start = (bf16[256,512]{1,0:T(8,128)(2,1)}, bf16[256,512]{1,0:T(8,128)(2,1)S(1)}, u32[]{:S(2)}, u32[]{:S(2)}) collective-permute-start(bf16[256,512]{1,0:T(8,128)(2,1)} %features.1), channel_id=1, source_target_pairs={{0,64},{32,96},{64,0},{96,32},{1,65},{33,97},{65,1},{97,33},{2,66}... | collective-permute-start | bytes 786440 | tf_op jit(solution)/shard_map/ppermute | solution.py:718
  5.1 11.2 %place_tiles.1.dense_hbm = bf16[8192,1024]{1,0:T(8,128)(2,1)} custom-call(s32[192]{0:T(256)} %rows.1, s32[192]{0:T(256)} %cols.1, s32[1]{0:T(128)S(6)} %copy.10.count, bf16[192,128,128]{2,1,0:T(8,128)(2,1)} %values.1), custom_call_target="tpu_custom_call" | custom-call | bytes 31457280 | tf_op jit(solution)/shard_map/place_tiles/pallas_call | solution.py:85
  16.3 0.0 collective-permute-done.features_across
  16.3 0.0 copy-start
  16.4 0.7 copy-done
  17.0 104.8 %layer.1 = (bf16[256,512]{1,0:T(8,128)(2,1)}, bf16[256,512]{1,0:T(8,128)(2,1)}, bf16[2,4,64,512]{3,2,1,0:T(8,128)(2,1)}) custom-call(bf16[256,512]{1,0:T(8,128)(2,1)} %features.1, bf16[256,512]{1,0:T(8,128)(2,1)} %copy-done, bf16[512,512]{1,0:T(8,128)(2,1)} %weight_hbm.1, bf16[8192,1024]{1,0:T(8,128)(2,1)} %place_tiles.1.dense_hbm, ...), custom_call_target="tpu_custom_call" | custom-call | tf_op jit(solution)/shard_map/layer/pallas_call | solution.py:616
  121.9 2.5 %finish.1 = (bf16[256,512]{1,0:T(8,128)(2,1)}, bf16[256,512]{1,0:T(8,128)(2,1)}, f32[512,512]{1,0:T(8,128)}) custom-call(bf16[256,512]{1,0:T(8,128)(2,1)} %get-tuple-element.6.first_in, bf16[256,512]{1,0:T(8,128)(2,1)} %get-tuple-element.7.second_in, bf16[512,512]{1,0:T(8,128)(2,1)} %bitcast.1), custom_call_target="tpu_custom_call" | custom-call | tf_op jit(solution)/shard_map/finish/pallas_call | solution.py:695
Async XLA Ops:
  0.6 15.7 %collective-permute-start = (bf16[256,512]{1,0:T(8,128)(2,1)}, bf16[256,512]{1,0:T(8,128)(2,1)S(1)}, u32[]{:S(2)}, u32[]{:S(2)}) collective-permute-start(bf16[256,512]{1,0:T(8,128)(2,1)} %features.1), channel_id=1, source_target_pairs={{0,64},{32,96},{64,0},{96,32},{1,65},{33,97},{65,1},{97,33},{2,66}... | collective-permute-start | bytes 786440 | tf_op jit(solution)/shard_map/ppermute | solution.py:718
  16.3 0.7 copy-start
